TPU v7x, 256 devices: a whole 4x4x8 slice. The times are simulated.
256 devices in a mesh: section: 8 (over x, core), tp: 32 (over y, z).
Axes of the slice: x: 4, y: 4, z: 8, core: 2. Of those that a mesh axis runs over, the one named last changes fastest.
Arguments:
- hidden: bfloat16 [8, 24, 8192], P('section', None, 'tp'), may hold values from -6 to 6
- attention_norm_scale: float32 [8192], replicated, may hold values from 0.1 to 1.9
- joined_projection_weight: bfloat16 [8, 8192, 10240], P('section', None, 'tp'), may hold values from -0.0625 to 0.0625
- adapter_down_weight: bfloat16 [8, 32, 8192, 64], P('section', 'tp'), may hold values from -0.0625 to 0.0625
- adapter_up_weight: bfloat16 [8, 32, 64, 10240], P('section', 'tp'), may hold values from -0.75 to 0.75
- cached_key_rows: bfloat16 [8, 24, 1024, 1024], P('section', None, 'tp'), may hold values from -180 to 180
- cached_value_rows: bfloat16 [8, 24, 1024, 1024], P('section', None, 'tp'), may hold values from -6 to 6
- row_adapter_index: int32 [8, 24, 1], P('section'), may hold values from 0 to 31; in each aligned block of 24 rows (0 to 23, 24 to 47, ..., all dimensions but the last counted through in order) at most 2 rows name the same one
- lengths: int32 [8, 24], P('section'), may hold values from 1 to 1023, 12288 in all within a row
Outputs:
- residual_out: bfloat16 [8, 24, 8192], P('section', None, 'tp')
- context: bfloat16 [8, 24, 8192], P('section', None, 'tp')
Inputs may be any that keep to these rules, and one draw needn't show every extreme that they name: `row_adapter_index`: in each section's batch at most 2 rows name the same adapter, a bound that some block reaches. The new token follows the used positions; the 24 lengths of one section's batch sum to 12288, and some row uses 1024 - 1 positions.
All inputs are finite; a program needn't handle non-finite values.
Results may differ from a plain program's by a relative error of at most 0.024.
Values may be sent and summed in bfloat16 or wider, within the bound.
No kernel may reach another device: no remote copies, remote signals or barrier semaphores. Data moves between devices by JAX's collectives and lax.ppermute only.
A program may use at most 128 MiB of HBM per device.

v0:
```python
import math

import jax
import jax.numpy as jnp
from jax import lax
from jax.sharding import PartitionSpec as P

H = 64
KVH = 8
HD = 128
QD = 8192
KVD = 1024


EPS = 1e-05
ADAPTER_SCALE = 0.5
NEGATIVE = -1e30


def combined_all(value, axis, join):
    pieces = jax.tree.map(lambda part: lax.all_gather(part, axis), value)
    head = jax.tree.map(lambda part: part[0], pieces)
    tail = jax.tree.map(lambda part: part[1:], pieces)
    total, _ = lax.scan(lambda total, piece: (join(total, piece), None), head, tail)
    return total


def passed_along(array, axis, by):
    devices = lax.axis_size(axis)
    return lax.ppermute(array, axis, [(i, (i + by) % devices) for i in range(devices)])


def combine_parts(first, second):
    top_a, total_a, mixed_a = first
    top_b, total_b, mixed_b = second
    top = jnp.maximum(top_a, top_b)
    scale_a = jnp.exp(top_a - top)
    scale_b = jnp.exp(top_b - top)
    return (
        top,
        total_a * scale_a + total_b * scale_b,
        mixed_a * scale_a[..., None] + mixed_b * scale_b[..., None],
    )


def on_device(
    hidden,
    attention_norm_scale,
    joined_projection_weight,
    adapter_down_weight,
    adapter_up_weight,
    cached_key_rows,
    cached_value_rows,
    row_adapter_index,
    lengths,
):
    width = lax.axis_size("tp")
    device = lax.axis_index("tp")
    rows_here = hidden[0]
    batch = rows_here.shape[0]
    gathered = lax.all_gather(rows_here, "tp", axis=1, tiled=True)
    wide = gathered.astype(jnp.float32)
    inverse = lax.rsqrt(jnp.mean(wide * wide, axis=-1, keepdims=True) + EPS)
    normed = (wide * inverse * attention_norm_scale).astype(jnp.bfloat16)
    base = jnp.dot(normed, joined_projection_weight[0], preferred_element_type=jnp.float32)
    chosen = row_adapter_index[0, :, 0]
    down_matrix = adapter_down_weight[0, 0]
    up_matrix = adapter_up_weight[0, 0]
    mine = (chosen == device)[:, None]
    reduced_rows = jnp.dot(normed, down_matrix, preferred_element_type=jnp.float32)
    reduced_rows = jnp.where(mine, reduced_rows, 0.0).astype(jnp.bfloat16)
    joined_update = (
        jnp.dot(reduced_rows, up_matrix, preferred_element_type=jnp.float32) * ADAPTER_SCALE
    )
    adapter_update = lax.psum_scatter(joined_update, "tp", scatter_dimension=1, tiled=True)
    joined_part = (base + adapter_update).astype(jnp.bfloat16)
    joined = lax.all_gather(joined_part, "tp", axis=1, tiled=True)
    groups = H // KVH
    queries = joined[:, :QD].reshape(batch, KVH, groups, HD)
    fresh_keys = joined[:, QD : QD + KVD].reshape(batch, KVH, HD)
    fresh_values = joined[:, QD + KVD :].reshape(batch, KVH, HD)
    span = cached_key_rows.shape[2]
    keys = cached_key_rows[0].reshape(batch, span, KVH, HD)
    values = cached_value_rows[0].reshape(batch, span, KVH, HD)
    factor = 1.0 / math.sqrt(HD)
    scores = (
        jnp.einsum("rkgd,rpkd->rkgp", queries, keys, preferred_element_type=jnp.float32) * factor
    )
    positions = device * span + jnp.arange(span, dtype=jnp.int32)
    valid = (positions[None, :] < lengths[0][:, None])[:, None, None, :]
    own_score = (
        jnp.einsum("rkgd,rkd->rkg", queries, fresh_keys, preferred_element_type=jnp.float32)
        * factor
    )
    keep_fresh = device == 0
    top = jnp.maximum(
        jnp.max(jnp.where(valid, scores, NEGATIVE), axis=-1),
        jnp.where(keep_fresh, own_score, NEGATIVE),
    )
    weights = jnp.where(valid, jnp.exp(scores - top[..., None]), 0.0)
    own_weight = jnp.where(keep_fresh, jnp.exp(own_score - top), 0.0)
    total = jnp.sum(weights, axis=-1) + own_weight
    mixed = jnp.einsum(
        "rkgp,rpkd->rkgd", weights.astype(jnp.bfloat16), values, preferred_element_type=jnp.float32
    )
    own_rounded = own_weight.astype(jnp.bfloat16).astype(jnp.float32)
    mixed = mixed + own_rounded[..., None] * fresh_values.astype(jnp.float32)[:, :, None, :]
    top = top.reshape(batch, H)
    total = total.reshape(batch, H)
    mixed = mixed.reshape(batch, H, HD)
    heads_here = H // width
    top_all, total_all, mixed_all = combined_all((top, total, mixed), "tp", combine_parts)
    result = mixed_all / total_all[..., None]
    result = lax.dynamic_slice_in_dim(result, device * heads_here, heads_here, 1)
    context_part = result.reshape(batch, heads_here * HD).astype(jnp.bfloat16)
    moved_rows, moved_context = passed_along((rows_here, context_part), "section", 1)
    return (moved_rows[None], moved_context[None])


def solution(mesh):
    return jax.shard_map(
        on_device,
        mesh=mesh,
        in_specs=(
            P("section", None, "tp"),
            P(),
            P("section", None, "tp"),
            P("section", "tp", None, None),
            P("section", "tp", None, None),
            P("section", None, "tp", None),
            P("section", None, "tp", None),
            P("section", None, None),
            P("section", None),
        ),
        out_specs=(P("section", None, "tp"), P("section", None, "tp")),
        check_vma=False,
    )
```

profile of v0, /device:TPU:32, one launch (start us, length us, event | category | flops | bytes accessed | tf_op | source)
XLA Modules:
  0.0 616.9 jit_solution(10712185240225633949)
XLA Ops:
  7.2 46.2 %all-gather = bf16[1,24,8192]{2,1,0:T(8,128)(2,1)S(1)} all-gather(bf16[1,24,256]{2,1,0:T(8,128)(2,1)} %param.11), channel_id=2, replica_groups=mesh['section'=8,'tp'=32] {'tp'}, dimensions={2}, use_global_device_ids=true | all-gather | bytes 405504 | tf_op jit(solution)/shard_map/all_gather | solution.py:61
  54.4 2.3 convolution_multiply_fusion
  56.7 3.1 copy.31
  59.9 1.8 copy.34
  61.8 3.1 copy.35
  65.0 217.5 %reduce-scatter.4.cloned.1.call-done = f32[320,24]{1,0:T(8,128)} async-done(((f32[10240,24]{1,0:T(8,128)}), f32[320,24]{1,0:T(8,128)}) %reduce-scatter.4.cloned.1.call-update) | async-done | bytes 30736
  283.5 4.0 fusion.25
  287.5 48.5 %all-gather.1 = bf16[32,320,24]{1,2,0:T(8,128)(2,1)S(1)} all-gather(bf16[1,320,24]{1,2,0:T(8,128)(2,1)S(1)} %fusion.25), channel_id=1, replica_groups=mesh['section'=8,'tp'=32] {'tp'}, dimensions={0}, use_global_device_ids=true | all-gather | bytes 506880 | tf_op jit(solution)/shard_map/all_gather | solution.py:77
  337.2 1.0 select_reduce_fusion
  339.7 1.5 fusion.16
  341.5 48.0 %all_gather.18 = f32[32,24,64]{2,1,0:T(8,128)S(1)} all-gather(f32[1,24,64]{2,1,0:T(8,128)S(1)} %copy.27), channel_id=1, replica_groups=mesh['section'=8,'tp'=32] {'tp'}, dimensions={0}, use_global_device_ids=true | all-gather | bytes 202752 | tf_op jit(solution)/shard_map/all_gather | solution.py:21
  389.6 49.4 %all_gather.17 = f32[32,24,64]{2,1,0:T(8,128)S(1)} all-gather(f32[1,24,64]{2,1,0:T(8,128)S(1)} %copy.25), channel_id=1, replica_groups=mesh['section'=8,'tp'=32] {'tp'}, dimensions={0}, use_global_device_ids=true | all-gather | bytes 202752 | tf_op jit(solution)/shard_map/all_gather | solution.py:21
  439.1 87.2 %all-gather.4.cloned.1.call-done = f32[32,24,64,128]{3,2,1,0:T(8,128)} async-done(((f32[1,24,64,128]{3,2,1,0:T(8,128)}), f32[32,24,64,128]{3,2,1,0:T(8,128)}) %all-gather.4.cloned.1.call-update) | async-done | bytes 25165840 | tf_op jit(solution)/shard_map/all_gather | solution.py:21
  526.3 17.4 %slice.44 = f32[31,24,64,128]{3,2,1,0:T(8,128)} slice(f32[32,24,64,128]{3,2,1,0:T(8,128)} %all-gather.4.cloned.1.call-done), slice={[1:32], [0:24], [0:64], [0:128]} | slice | bytes 48758784 | tf_op jit(solution)/shard_map/slice | solution.py:23
  543.8 1.2 slice_bitcast_fusion
  544.9 59.3 %while.14 = (s32[]{:T(128)}, f32[24,64]{1,0:T(8,128)S(1)}, f32[24,64]{1,0:T(8,128)S(1)}, f32[24,64,128]{2,1,0:T(8,128)S(1)}, f32[31,24,64]{2,1,0:T(8,128)S(1)}, ...) while((s32[]{:T(128)}, f32[24,64]{1,0:T(8,128)S(1)}, f32[24,64]{1,0:T(8,128)S(1)}, ...), condition=%wide.region_5.6_spmd, body=%wide.region_4.5_spmd.sunk | while | flops 599042 | bytes 2420829 | solution.py:24
  545.0 1.9 fusion.57
  546.9 1.9 fusion.57
  548.8 1.9 fusion.57
  550.7 1.9 fusion.57
  552.6 1.9 fusion.57
  554.6 1.9 fusion.57
  556.5 1.9 fusion.57
  558.4 1.9 fusion.57
  560.3 1.9 fusion.57
  562.2 1.9 fusion.57
  564.1 1.9 fusion.57
  566.0 1.9 fusion.57
  567.9 1.9 fusion.57
  569.9 1.9 fusion.57
  571.8 1.9 fusion.57
  573.7 1.9 fusion.57
  575.6 1.9 fusion.57
  577.5 1.9 fusion.57
  579.4 1.9 fusion.57
  581.3 1.9 fusion.57
  583.3 1.9 fusion.57
  585.2 1.9 fusion.57
  587.1 1.9 fusion.57
  589.0 1.9 fusion.57
  590.9 1.9 fusion.57
  592.8 1.9 fusion.57
  594.7 1.9 fusion.57
  596.6 1.9 fusion.57
  598.6 1.9 fusion.57
  600.5 1.9 fusion.57
  602.4 1.9 fusion.57
  604.5 4.3 collective-permute-done.1
  (80 shorter events, 7.2 us)
Async XLA Ops:
  7.2 47.2 %copy-start = (bf16[1,1,64,10240]{3,2,1,0:T(8,128)(2,1)S(1)}, bf16[1,1,64,10240]{3,2,1,0:T(8,128)(2,1)}, u32[]{:S(2)}) copy-start(bf16[1,1,64,10240]{3,2,1,0:T(8,128)(2,1)} %param.15) | copy-start | bytes 3932164
  7.2 275.3 %reduce-scatter.4.cloned.1.call-start = ((), (), s32[]{:S(2)}) async-start(), calls=%async_computation.2 | async-start | bytes 5406720
  59.9 466.4 %all-gather.4.cloned.1.call-start = ((), (), s32[]{:S(2)}) async-start(), calls=%async_computation.1 | async-start | bytes 25952256 | tf_op jit(solution)/shard_map/all_gather | solution.py:21
  61.8 3.1 copy-start.5
  61.8 221.7 %copy-start.3 = (f32[8192]{0:T(1024)S(1)}, f32[8192]{0:T(1024)}, u32[]{:S(2)}) copy-start(f32[8192]{0:T(1024)} %param.12) | copy-start | bytes 98308
  338.3 1.4 copy-start.2
  339.7 1.6 copy-start.4
  341.3 263.2 %collective-permute-start = (bf16[24,256]{1,0:T(8,128)(2,1)S(1)}, bf16[24,256]{1,0:T(8,128)(2,1)S(1)}, u32[]{:S(2)}, u32[]{:S(2)}) collective-permute-start(bf16[24,256]{1,0:T(8,128)(2,1)S(1)} %bitcast.109), channel_id=1, source_target_pairs={{0,32},{32,64},{64,96},{96,128},{128,160},{160,192},{192,224},{224... | collective-permute-start | bytes 36872 | tf_op jit(solution)/shard_map/ppermute | solution.py:30
  604.3 5.8 copy-start.1
  604.5 4.3 collective-permute-start.1
Sparse Core Ops, SparseCore 0:
  60.0 222.4 reduce-scatter.3
  341.4 184.9 all-gather.3
where the time goes:
time: 620 us; the launch traced here: 617 us
  waiting for transfers between devices  309 us (50%)
  blocking collectives  192 us (31%)
  other arithmetic  60.2 us (10%)
  local copies, waits for them, and re-layouts  31 us (5%)
  between operations  14.3 us (2%)
  matrix products  9.22 us (1%)
    unnamed x3, waiting for transfers between devices  218 us
    all_gather x2, blocking collectives, combined_all(): pieces = jax.tree.map(lambda part: lax.all_gather(part, axis), value)  97.4 us
    all_gather x1, waiting for transfers between devices, combined_all(): pieces = jax.tree.map(lambda part: lax.all_gather(part, axis), value)  87.2 us
    add x31, other arithmetic, combine_parts(): mixed_a * scale_a[..., None] + mixed_b * scale_b[..., None]  57.8 us
    all_gather x1, blocking collectives, on_device(): joined = lax.all_gather(joined_part, 'tp', axis=1, tiled=True)  48.5 us
    all_gather x1, blocking collectives, on_device(): gathered = lax.all_gather(rows_here, 'tp', axis=1, tiled=True)  46.2 us
    slice x3, local copies, waits for them, and re-layouts, combined_all(): tail = jax.tree.map(lambda part: part[1:], pieces)  17.5 us
  transfers between devices with their start and end apart: 4, of which 3 were waited for; matrix products, arithmetic and copies ran while one was open for 13% of the time, Pallas kernels for 0%

commit v1 on v0

v1 whole, which is shorter than its diff:
```python
import math

import jax
import jax.numpy as jnp
from jax import lax
from jax.experimental import pallas as pl
from jax.experimental.pallas import tpu as pltpu
from jax.sharding import PartitionSpec as P

H = 64
KVH = 8
HD = 128
MOST = 2
ROWS = 24
TP = 32
SPAN = 32
QUAD = 4
HEADS_HERE = H // TP
OWN = ROWS * HEADS_HERE
SLOT = 64
PART = 56

EPS = 1e-05
ADAPTER_SCALE = 0.5
NEGATIVE = -1e30
FLOOR = -1e20
FACTOR = 1.0 / math.sqrt(HD)


def passed_along(array, axis, by):
    devices = lax.axis_size(axis)
    return lax.ppermute(array, axis, [(i, (i + by) % devices) for i in range(devices)])


def to_all(piece, width):
    copies = jnp.broadcast_to(piece[None], (width,) + piece.shape)
    return lax.all_to_all(copies, "tp", 0, 0)


def on_vmem(kernel, mebibytes, out_shape, scratch, *arguments):
    vmem = pl.BlockSpec(memory_space=pltpu.VMEM)
    return pl.pallas_call(
        kernel,
        out_shape=out_shape,
        in_specs=[vmem if a.dtype != jnp.int32 else pl.BlockSpec(memory_space=pltpu.SMEM) for a in arguments],
        out_specs=jax.tree.map(lambda _: vmem, out_shape),
        scratch_shapes=scratch,
        compiler_params=pltpu.CompilerParams(vmem_limit_bytes=mebibytes * 1024 * 1024),
    )(*arguments)


def low_lanes(shape):
    return lax.broadcasted_iota(jnp.int32, shape, len(shape) - 1) < HD // 2


def pack_kernel(device_ref, base_ref, spread_ref, received_ref, slots_ref):
    received = received_ref[...].reshape(TP * 8, HD)
    tiles = []
    for k in range(3):
        change = jnp.dot(spread_ref[k], received, preferred_element_type=jnp.float32)
        tiles.append(base_ref[:, k * HD : (k + 1) * HD] + change)
    odd = device_ref[0] % 2 == 1
    turned = [pltpu.roll(tile, HD // 2, 1) for tile in tiles]
    low = low_lanes((ROWS, HD))
    first = jnp.where(odd, jnp.where(low, turned[0], turned[1]), tiles[0])
    second = jnp.where(odd, jnp.where(low, turned[1], turned[2]), tiles[1])
    part = jnp.where(odd, tiles[0], tiles[2])
    turned_part = jnp.where(odd, turned[0], turned[2])
    low = low_lanes((8, HD))
    even_pair = jnp.where(low, part[0:8], turned_part[8:16])
    odd_pair = jnp.where(low, part[8:16], turned_part[0:8])
    pair = jnp.where(odd, odd_pair, even_pair)
    last = jnp.where(odd, turned_part[16:24], part[16:24])
    slot = jnp.concatenate([first, second, pair, last], axis=0).astype(jnp.bfloat16)
    for t in range(TP):
        slots_ref[t] = slot


def attention_kernel(device_ref, slots_ref, keys_ref, values_ref, bias_ref, sent_ref, own_ref, own_value_ref, query, fresh, result, levels):
    low = low_lanes((8, HD))

    def put(head, rows):
        if head < H:
            query[head // 2, pl.ds(head % 2, ROWS, stride=2), :] = rows
        else:
            fresh[head - H, pl.ds(0, ROWS, stride=2), :] = rows
            fresh[head - H, pl.ds(1, ROWS, stride=2), :] = rows

    for p in range(TP // 2):
        even = slots_ref[2 * p].astype(jnp.float32)
        odd = slots_ref[2 * p + 1].astype(jnp.float32)
        put(5 * p, even[0:24])
        put(5 * p + 1, even[24:48])
        middle = jnp.where(low, odd[48:56], even[48:56])
        put(
            5 * p + 2,
            jnp.concatenate(
                [
                    jnp.where(low, even[48:56], odd[48:56]),
                    pltpu.roll(middle, HD // 2, 1),
                    jnp.where(low, even[56:64], odd[56:64]),
                ],
                axis=0,
            ),
        )
        put(5 * p + 3, odd[0:24])
        put(5 * p + 4, odd[24:48])

    device = device_ref[0]
    group = device // (TP // KVH)
    own_level = jnp.sum(query[device] * fresh[group], axis=1, keepdims=True) * FACTOR
    own_ref[...] = jnp.broadcast_to(own_level, (OWN, HD))
    own_value_ref[...] = fresh[KVH + group]

    quads = ROWS // QUAD
    rows = QUAD * SPAN
    lane = lax.broadcasted_iota(jnp.int32, (HD, HD), 1)
    for gg in range(2):
        for q in range(quads):
            left = jnp.concatenate([query[16 * gg + j, 8 * q : 8 * q + 8, :] for j in range(16)], axis=0)
            turned = jnp.transpose(left)
            parts = [jnp.where(lane // 32 == i, turned, 0.0).astype(jnp.bfloat16) for i in range(4)]
            right = jnp.concatenate(parts, axis=0)
            keys = keys_ref[QUAD * q : QUAD * (q + 1), :, 512 * gg : 512 * (gg + 1)].reshape(rows, 512)
            scores = jnp.dot(keys, right, preferred_element_type=jnp.float32) * FACTOR + bias_ref[q]
            top = jnp.maximum(jnp.max(scores, axis=0, keepdims=True), FLOOR)
            weights = jnp.exp(scores - top)
            total = jnp.sum(weights, axis=0, keepdims=True)
            some = total > 0.0
            safe = jnp.where(some, total, 1.0)
            levels[gg, q : q + 1, :] = jnp.where(some, top + jnp.log(safe), NEGATIVE)
            weights = jnp.transpose(weights * (1.0 / safe)).astype(jnp.bfloat16)
            for i in range(4):
                g = 4 * gg + i
                values = values_ref[QUAD * q : QUAD * (q + 1), :, g * HD : (g + 1) * HD].reshape(rows, HD)
                mixed = jnp.dot(weights[32 * i : 32 * i + 32], values, preferred_element_type=jnp.float32)
                for j in range(4):
                    result[4 * g + j, 8 * q : 8 * q + 8, :] = mixed[8 * j : 8 * j + 8]
    sub = lax.broadcasted_iota(jnp.int32, (8, HD), 0)
    diagonal = lax.broadcasted_iota(jnp.int32, (8, HD), 1) // 8 == sub
    for gg in range(2):
        slanted = pltpu.roll(levels[gg], 0, 1, stride=8, stride_axis=0)
        for j in range(16):
            line = pltpu.roll(slanted, (HD - 8 * j) % HD, 1) if j else slanted
            line = jnp.sum(jnp.where(diagonal & (sub < quads), line, 0.0), axis=0, keepdims=True)
            high = line.astype(jnp.bfloat16).astype(jnp.float32)
            middle = (line - high).astype(jnp.bfloat16).astype(jnp.float32)
            rest = line - high - middle
            lines = jnp.where(sub == 0, high, jnp.where(sub == 1, middle, jnp.where(sub == 2, rest, 0.0)))
            t = 16 * gg + j
            sent_ref[t] = jnp.concatenate([result[t], lines], axis=0).astype(jnp.bfloat16)


def combine_kernel(arrived_ref, own_ref, own_value_ref, context_ref):
    eye = lax.broadcasted_iota(jnp.int32, (OWN, HD), 0) == lax.broadcasted_iota(jnp.int32, (OWN, HD), 1)
    own_level = jnp.sum(jnp.where(eye, own_ref[...], 0.0), axis=0, keepdims=True)
    lines = []
    for t in range(TP):
        terms = arrived_ref[t].astype(jnp.float32)[OWN:PART]
        lines.append(jnp.sum(terms, axis=0, keepdims=True))
    levels = jnp.concatenate(lines, axis=0)
    highest = jnp.maximum(jnp.max(levels, axis=0, keepdims=True), own_level)
    shares = jnp.exp(levels - highest)
    own_share = jnp.exp(own_level - highest)
    whole = jnp.sum(shares, axis=0, keepdims=True) + own_share
    own_share = jnp.broadcast_to(own_share / whole, (8, HD))
    shares = jnp.concatenate([shares / whole, own_share], axis=0)
    columns = jnp.transpose(jnp.concatenate([shares, jnp.zeros((HD - TP - 8, HD), jnp.float32)], axis=0))
    total = columns[0:OWN, TP : TP + 1] * own_value_ref[...]
    for t in range(TP):
        total = total + columns[0:OWN, t : t + 1] * arrived_ref[t].astype(jnp.float32)[0:OWN]
    context_ref[...] = total


def on_device(
    hidden,
    attention_norm_scale,
    joined_projection_weight,
    adapter_down_weight,
    adapter_up_weight,
    cached_key_rows,
    cached_value_rows,
    row_adapter_index,
    lengths,
):
    width = lax.axis_size("tp")
    device = lax.axis_index("tp")
    where = device.astype(jnp.int32).reshape(1)
    rows_here = hidden[0]
    batch, features = rows_here.shape
    moved_rows = passed_along(rows_here, "section", 1)

    chosen = row_adapter_index[0, :, 0]
    same = chosen[:, None] == chosen[None, :]
    earlier = jnp.arange(batch)[None, :] < jnp.arange(batch)[:, None]
    place = jnp.sum(same & earlier, axis=1)
    slots = jnp.arange(MOST)
    mine = (chosen[None, :] == device) & (place[None, :] == slots[:, None])
    slot_of_row = chosen * 8 + place * 3
    lines = slot_of_row[None, :, None] + jnp.arange(3)[:, None, None]
    spread = (lines == jnp.arange(width * 8)[None, None, :]).astype(jnp.bfloat16)

    span = cached_key_rows.shape[2]
    used = lengths[0].reshape(batch // QUAD, QUAD, 1, 1, 1, 1)
    seen = device * span + jnp.arange(span, dtype=jnp.int32).reshape(span, 1, 1, 1) < used
    seen = seen & jnp.eye(QUAD, dtype=bool).reshape(1, QUAD, 1, 1, QUAD, 1)
    bias = jnp.where(seen, 0.0, NEGATIVE).astype(jnp.float32)
    bias = jnp.broadcast_to(bias, (batch // QUAD, QUAD, span, 16, QUAD, HEADS_HERE))
    bias = bias.reshape(batch // QUAD, QUAD * span, HD)

    pieces = to_all(rows_here, width)
    gathered = pieces.transpose(1, 0, 2).reshape(batch, width * features)
    wide = gathered.astype(jnp.float32)
    inverse = lax.rsqrt(jnp.mean(wide * wide, axis=-1, keepdims=True) + EPS)
    normed = (wide * inverse * attention_norm_scale).astype(jnp.bfloat16)
    reduced_rows = jnp.dot(normed, adapter_down_weight[0, 0], preferred_element_type=jnp.float32)
    picked = jnp.dot(
        mine.astype(jnp.bfloat16),
        reduced_rows.astype(jnp.bfloat16),
        preferred_element_type=jnp.float32,
    ).astype(jnp.bfloat16)
    update = jnp.dot(picked, adapter_up_weight[0, 0], preferred_element_type=jnp.float32)
    columns = update.shape[1] // width
    update = (update * ADAPTER_SCALE).astype(jnp.bfloat16).reshape(MOST, width, columns)
    update = jnp.pad(update.transpose(1, 0, 2), ((0, 0), (0, 0), (0, 3 * HD - columns)))
    update = jnp.pad(update.reshape(width, 3 * MOST, HD), ((0, 0), (0, 8 - 3 * MOST), (0, 0)))
    received = lax.all_to_all(update, "tp", 0, 0)
    base = jnp.dot(normed, joined_projection_weight[0], preferred_element_type=jnp.float32)
    base = jnp.pad(base, ((0, 0), (0, 3 * HD - columns)))
    slots = on_vmem(
        pack_kernel,
        4,
        jax.ShapeDtypeStruct((TP, SLOT, HD), jnp.bfloat16),
        [],
        where,
        base,
        spread,
        received,
    )
    joined = lax.all_to_all(slots, "tp", 0, 0)

    sent, own, own_value = on_vmem(
        attention_kernel,
        12,
        (
            jax.ShapeDtypeStruct((TP, PART, HD), jnp.bfloat16),
            jax.ShapeDtypeStruct((OWN, HD), jnp.float32),
            jax.ShapeDtypeStruct((OWN, HD), jnp.float32),
        ),
        [
            pltpu.VMEM((TP, OWN, HD), jnp.float32),
            pltpu.VMEM((2 * KVH, OWN, HD), jnp.float32),
            pltpu.VMEM((TP, OWN, HD), jnp.float32),
            pltpu.VMEM((2, 8, HD), jnp.float32),
        ],
        where,
        joined,
        cached_key_rows[0],
        cached_value_rows[0],
        bias,
    )
    arrived = lax.all_to_all(sent, "tp", 0, 0)
    context = on_vmem(
        combine_kernel, 4, jax.ShapeDtypeStruct((OWN, HD), jnp.float32), [], arrived, own, own_value
    )
    context = context.reshape(batch, HEADS_HERE * HD).astype(jnp.bfloat16)
    moved_context = passed_along(context, "section", 1)
    return (moved_rows[None], moved_context[None])


def solution(mesh):
    return jax.shard_map(
        on_device,
        mesh=mesh,
        in_specs=(
            P("section", None, "tp"),
            P(),
            P("section", None, "tp"),
            P("section", "tp", None, None),
            P("section", "tp", None, None),
            P("section", None, "tp", None),
            P("section", None, "tp", None),
            P("section", None, None),
            P("section", None),
        ),
        out_specs=(P("section", None, "tp"), P("section", None, "tp")),
        check_vma=False,
    )
```

time: 620 us -> 100 us (0.16)
  waiting for transfers between devices: 309 us -> 44.2 us
  blocking collectives: 192 us -> 0 us
  other arithmetic: 60.2 us -> 3.55 us
  starting transfers between devices: 0.11 us -> 25.7 us
  local copies, waits for them, and re-layouts: 31 us -> 14.7 us
  between operations: 14.3 us -> 0.86 us
    unnamed x3 -> x0, waiting for transfers between devices: 218 us -> none
    all_gather x4 -> x0, blocking collectives: 192 us -> none  [the longest x2 97.4 us: combined_all(): pieces = jax.tree.map(lambda part: lax.all_gather(part, axis), value)]
    all_gather x1 -> x0, waiting for transfers between devices: 87.2 us -> none  [combined_all(): pieces = jax.tree.map(lambda part: lax.all_gather(part, axis), value)]
    add x63 -> x3, other arithmetic: 58.5 us -> 0.67 us  [the longest x2 0.67 us: on_device(): lines = slot_of_row[None, :, None] + jnp.arange(3)[:, None, None]]
    all_to_all x0 -> x4, waiting for transfers between devices: none -> 39.9 us  [the longest x1 14.4 us: on_device(): arrived = lax.all_to_all(sent, 'tp', 0, 0)]
    all_to_all x0 -> x4, starting transfers between devices: none -> 25.7 us  [the longest x1 11.4 us: to_all(): return lax.all_to_all(copies, 'tp', 0, 0)]
    slice x3 -> x0, local copies, waits for them, and re-layouts: 17.5 us -> none  [combined_all(): tail = jax.tree.map(lambda part: part[1:], pieces)]
    unnamed x23 -> x19, local copies, waits for them, and re-layouts: 11.8 us -> 4.91 us
  transfers between devices with their start and end apart: 4 -> 6, of which waited for: 3 -> 5; matrix products, arithmetic and copies ran while one was open for 13% -> 15% of each run, Pallas kernels for 0% -> 1%
where the time goes in v1:
time: 100 us; the launch traced here: 99.5 us
  waiting for transfers between devices  44.2 us (44%)
  starting transfers between devices  25.7 us (26%)
  local copies, waits for them, and re-layouts  14.7 us (15%)
  Pallas kernels  5.65 us (6%)
  matrix products  4.79 us (5%)
  other arithmetic  3.55 us (4%)
    all_to_all x1, waiting for transfers between devices, on_device(): arrived = lax.all_to_all(sent, 'tp', 0, 0)  14.4 us
    all_to_all x1, waiting for transfers between devices, to_all(): return lax.all_to_all(copies, 'tp', 0, 0)  11.8 us
    all_to_all x1, starting transfers between devices, to_all(): return lax.all_to_all(copies, 'tp', 0, 0)  11.4 us
    all_to_all x1, waiting for transfers between devices, on_device(): joined = lax.all_to_all(slots, 'tp', 0, 0)  8.69 us
    pallas_call x3, Pallas kernels, on_vmem(): pl.pallas_call(kernel, out_shape=out_shape, in_specs=[vmem if a.dtype !=...  5.65 us
    all_to_all x1, waiting for transfers between devices, on_device(): received = lax.all_to_all(update, 'tp', 0, 0)  5.08 us
    unnamed x19, local copies, waits for them, and re-layouts  4.91 us
    reshape x2, local copies, waits for them, and re-layouts, on_device(): bias = bias.reshape(batch // QUAD, QUAD * span, HD)  4.87 us
  transfers between devices with their start and end apart: 6, of which 5 were waited for; matrix products, arithmetic and copies ran while one was open for 15% of the time, Pallas kernels for 1%

profile of v1, /device:TPU:32, one launch (start us, length us, event | category | flops | bytes accessed | tf_op | source)
XLA Modules:
  0.0 99.5 jit_solution(11406872424525234821)
XLA Ops:
  0.6 0.0 copy-start
  0.6 0.0 copy-start.5
  0.7 1.6 %broadcast_in_dim.17 = bf16[32,24,256]{2,1,0:T(8,128)(2,1)} broadcast(bf16[24,256]{1,0:T(8,128)(2,1)} %bitcast.41), dimensions={1,2} | broadcast | bytes 405504 | tf_op jit(solution)/shard_map/broadcast_in_dim | solution.py:36
  2.3 11.4 %all-to-all-start = ((bf16[32,24,256]{2,1,0:T(8,128)(2,1)}), bf16[32,24,256]{2,1,0:T(8,128)(2,1)S(1)}, u32[]{:S(2)}, u32[]{:S(2)}) async-start(bf16[32,24,256]{2,1,0:T(8,128)(2,1)} %broadcast_in_dim.17), calls=%async_computation | async-start | bytes 786432 | tf_op jit(solution)/shard_map/all_to_all | solution.py:37
  13.7 0.8 mul.58
  14.4 0.7 broadcast_compare_fusion.1
  15.1 0.9 convert_reduce_fusion
  16.0 0.7 fusion.18
  16.7 0.1 fusion.12.spread_ref
  16.8 11.8 %all-to-all-done = bf16[32,24,256]{2,1,0:T(8,128)(2,1)S(1)} async-done(((bf16[32,24,256]{2,1,0:T(8,128)(2,1)}), bf16[32,24,256]{2,1,0:T(8,128)(2,1)S(1)}, u32[]{:S(2)}, u32[]{:S(2)}) %all-to-all-start) | async-done | bytes 393248 | tf_op jit(solution)/shard_map/all_to_all | solution.py:37
  28.5 0.2 fusion.8
  28.8 0.2 fusion.11
  29.0 0.0 copy-done.5
  29.0 0.5 fusion.5
  29.5 0.0 copy-done
  29.5 0.3 fusion
  29.8 0.1 reshape.123
  30.1 0.6 pad.14
  30.7 4.8 %all-to-all-start.1 = ((bf16[32,8,128]{2,1,0:T(8,128)(2,1)}), bf16[32,8,128]{2,1,0:T(8,128)(2,1)S(1)}, u32[]{:S(2)}, u32[]{:S(2)}) async-start(bf16[32,8,128]{2,1,0:T(8,128)(2,1)} %pad.14), calls=%async_computation.1 | async-start | bytes 131072 | tf_op jit(solution)/shard_map/all_to_all | solution.py:227
  35.5 4.0 %fusion.1 = f32[24,320]{1,0:T(8,128)S(1)} fusion(bf16[24,8192]{1,0:T(8,128)(2,1)S(1)} %bitcast.39, bf16[1,8192,320]{1,2,0:T(8,128)(2,1)} %param.11), kind=kOutput, calls=%fused_computation.2 | convolution fusion | flops 125829120 | bytes 5666816 | tf_op jit(solution)/shard_map/dot_general | solution.py:228
  39.5 0.0 copy-start.7
  39.5 5.1 %all-to-all-done.1.received_ref = bf16[32,8,128]{2,1,0:T(8,128)(2,1)S(1)} async-done(((bf16[32,8,128]{2,1,0:T(8,128)(2,1)}), bf16[32,8,128]{2,1,0:T(8,128)(2,1)S(1)}, u32[]{:S(2)}, u32[]{:S(2)}) %all-to-all-start.1) | async-done | bytes 65568 | tf_op jit(solution)/shard_map/all_to_all | solution.py:227
  44.6 1.1 %shard_map.104 = bf16[32,64,128]{2,1,0:T(8,128)(2,1)} custom-call(s32[1]{0:T(128)} %bitcast.2.device_ref, f32[24,384]{1,0:T(8,128)S(1)} %pad.12.base_ref, bf16[3,24,256]{2,1,0:T(8,128)(2,1)S(1)} %fusion.12.spread_ref, bf16[32,8,128]{2,1,0:T(8,128)(2,1)S(1)} %all-to-all-done.1.received_ref), custom_call_target="tpu_custom_call" | custom-call | tf_op jit(solution)/shard_map/pallas_call | solution.py:42
  45.6 4.7 %all-to-all-start.2 = ((bf16[32,64,128]{2,1,0:T(8,128)(2,1)}), bf16[32,64,128]{2,1,0:T(8,128)(2,1)S(1)}, u32[]{:S(2)}, u32[]{:S(2)}) async-start(bf16[32,64,128]{2,1,0:T(8,128)(2,1)} %shard_map.104), calls=%async_computation.2 | async-start | bytes 1048576 | tf_op jit(solution)/shard_map/all_to_all | solution.py:240
  50.4 0.5 broadcast.123
  50.9 0.0 copy-done.7
  50.9 0.7 reduce.5
  51.5 0.1 lt.37
  51.6 0.1 broadcast_compare_fusion
  51.7 0.1 and_select_fusion
  51.8 1.5 %broadcast_in_dim.20 = f32[6,4,32,16,4,2]{2,1,5,4,3,0:T(4,128)} broadcast(f32[6,4,32,4]{2,1,3,0:T(4,128)S(1)} %and_select_fusion), dimensions={0,1,2,4} | broadcast | bytes 405504 | tf_op jit(solution)/shard_map/broadcast_in_dim | solution.py:208
  53.3 3.0 %reshape.125 = f32[6,128,128]{1,2,0:T(8,128)} reshape(f32[6,4,32,16,4,2]{2,1,5,4,3,0:T(4,128)} %broadcast_in_dim.20) | data formatting | bytes 786432 | tf_op jit(solution)/shard_map/reshape | solution.py:209
  56.3 1.9 %copy.19.bias_ref = f32[6,128,128]{2,1,0:T(8,128)} copy(f32[6,128,128]{1,2,0:T(8,128)} %reshape.125) | data formatting | bytes 786432 | tf_op jit(solution)/shard_map/reshape | solution.py:209
  58.2 8.7 %all-to-all-done.2.slots_ref = bf16[32,64,128]{2,1,0:T(8,128)(2,1)S(1)} async-done(((bf16[32,64,128]{2,1,0:T(8,128)(2,1)}), bf16[32,64,128]{2,1,0:T(8,128)(2,1)S(1)}, u32[]{:S(2)}, u32[]{:S(2)}) %all-to-all-start.2) | async-done | bytes 524320 | tf_op jit(solution)/shard_map/all_to_all | solution.py:240
  66.9 0.0 copy-done.1
  66.9 1.4 %copy-done.2 = bf16[1,24,32,1024]{3,2,1,0:T(8,128)(2,1)S(1)} copy-done((bf16[1,24,32,1024]{3,2,1,0:T(8,128)(2,1)S(1)}, bf16[1,24,32,1024]{3,2,1,0:T(8,128)(2,1)}, u32[]{:S(2)}) %copy-start.2) | copy-done | bytes 1572888
  68.3 1.0 copy-done.3
  69.3 4.1 %shard_map.105 = (bf16[32,56,128]{2,1,0:T(8,128)(2,1)S(1)}, f32[48,128]{1,0:T(8,128)S(1)}, f32[48,128]{1,0:T(8,128)S(1)}) custom-call(s32[1]{0:T(128)} %bitcast.2.device_ref, bf16[32,64,128]{2,1,0:T(8,128)(2,1)S(1)} %all-to-all-done.2.slots_ref, bf16[24,32,1024]{2,1,0:T(8,128)(2,1)S(1)} %bitcast.36, bf16[24,32,1024]{2,1,0:T(8,128)(2,1)S(1)} %bitcast.37, ...), custom_call_target="tpu_custom_call" | custom-call | tf_op jit(solution)/shard_map/pallas_call | solution.py:42
  73.4 0.8 copy-done.4
  74.2 4.8 %all-to-all-start.3 = ((bf16[32,56,128]{2,1,0:T(8,128)(2,1)}), bf16[32,56,128]{2,1,0:T(8,128)(2,1)S(1)}, u32[]{:S(2)}, u32[]{:S(2)}) async-start(bf16[32,56,128]{2,1,0:T(8,128)(2,1)} %copy-done.4), calls=%async_computation.3 | async-start | bytes 917504 | tf_op jit(solution)/shard_map/all_to_all | solution.py:262
  79.0 0.0 collective-permute-start
  79.0 14.4 %all-to-all-done.3.arrived_ref = bf16[32,56,128]{2,1,0:T(8,128)(2,1)S(1)} async-done(((bf16[32,56,128]{2,1,0:T(8,128)(2,1)}), bf16[32,56,128]{2,1,0:T(8,128)(2,1)S(1)}, u32[]{:S(2)}, u32[]{:S(2)}) %all-to-all-start.3) | async-done | bytes 458784 | tf_op jit(solution)/shard_map/all_to_all | solution.py:262
  93.4 0.5 shard_map.106
  93.9 0.0 collective-permute-start.1
  94.0 0.0 collective-permute-done
  94.0 4.3 %collective-permute-done.1 = bf16[24,256]{1,0:T(8,128)(2,1)S(1)} collective-permute-done((bf16[24,256]{1,0:T(8,128)(2,1)S(1)}, bf16[24,256]{1,0:T(8,128)(2,1)S(1)}, u32[]{:S(2)}, u32[]{:S(2)}) %collective-permute-start.1) | collective-permute-done | bytes 12320 | tf_op jit(solution)/shard_map/ppermute | solution.py:32
  98.3 0.6 copy.25
  98.9 0.6 copy.26
  (17 shorter events, 0.2 us)
Async XLA Ops:
  0.6 28.9 %copy-start = (bf16[1,1,64,10240]{3,2,1,0:T(8,128)(2,1)S(1)}, bf16[1,1,64,10240]{3,2,1,0:T(8,128)(2,1)}, u32[]{:S(2)}) copy-start(bf16[1,1,64,10240]{3,2,1,0:T(8,128)(2,1)} %param.13) | copy-start | bytes 3932164
  0.6 28.3 %copy-start.5 = (bf16[1,1,8192,64]{2,3,1,0:T(8,128)(2,1)S(1)}, bf16[1,1,8192,64]{2,3,1,0:T(8,128)(2,1)}, u32[]{:S(2)}) copy-start(bf16[1,1,8192,64]{2,3,1,0:T(8,128)(2,1)} %param.12) | copy-start | bytes 3145732
  2.3 26.2 %all-to-all-start = ((bf16[32,24,256]{2,1,0:T(8,128)(2,1)}), bf16[32,24,256]{2,1,0:T(8,128)(2,1)S(1)}, u32[]{:S(2)}, u32[]{:S(2)}) async-start(bf16[32,24,256]{2,1,0:T(8,128)(2,1)} %broadcast_in_dim.17), calls=%async_computation | async-start | bytes 786432 | tf_op jit(solution)/shard_map/all_to_all | solution.py:37
  30.7 13.9 %all-to-all-start.1 = ((bf16[32,8,128]{2,1,0:T(8,128)(2,1)}), bf16[32,8,128]{2,1,0:T(8,128)(2,1)S(1)}, u32[]{:S(2)}, u32[]{:S(2)}) async-start(bf16[32,8,128]{2,1,0:T(8,128)(2,1)} %pad.14), calls=%async_computation.1 | async-start | bytes 131072 | tf_op jit(solution)/shard_map/all_to_all | solution.py:227
  39.5 11.4 %copy-start.7 = (s32[1,24]{1,0:T(1,128)S(1)}, s32[1,24]{1,0:T(1,128)}, u32[]{:S(2)}) copy-start(s32[1,24]{1,0:T(1,128)} %param.17) | copy-start | bytes 292
  45.6 21.2 %all-to-all-start.2 = ((bf16[32,64,128]{2,1,0:T(8,128)(2,1)}), bf16[32,64,128]{2,1,0:T(8,128)(2,1)S(1)}, u32[]{:S(2)}, u32[]{:S(2)}) async-start(bf16[32,64,128]{2,1,0:T(8,128)(2,1)} %shard_map.104), calls=%async_computation.2 | async-start | bytes 1048576 | tf_op jit(solution)/shard_map/all_to_all | solution.py:240
  53.3 13.6 %copy-start.1 = (bf16[1,24,32,1024]{3,2,1,0:T(8,128)(2,1)S(1)}, bf16[1,24,32,1024]{3,2,1,0:T(8,128)(2,1)}, u32[]{:S(2)}) copy-start(bf16[1,24,32,1024]{3,2,1,0:T(8,128)(2,1)} %param.14) | copy-start | bytes 4718596
  66.9 1.4 %copy-start.2 = (bf16[1,24,32,1024]{3,2,1,0:T(8,128)(2,1)S(1)}, bf16[1,24,32,1024]{3,2,1,0:T(8,128)(2,1)}, u32[]{:S(2)}) copy-start(bf16[1,24,32,1024]{3,2,1,0:T(8,128)(2,1)} %param.15) | copy-start | bytes 4718596
  68.3 1.0 %copy-start.3 = (f32[6,128,128]{2,1,0:T(8,128)S(1)}, f32[6,128,128]{2,1,0:T(8,128)}, u32[]{:S(2)}) copy-start(f32[6,128,128]{2,1,0:T(8,128)} %copy.19.bias_ref) | copy-start | bytes 1179652
  69.3 9.7 %copy-start.6 = (bf16[1,24,256]{2,1,0:T(8,128)(2,1)S(1)}, bf16[1,24,256]{2,1,0:T(8,128)(2,1)}, u32[]{:S(2)}) copy-start(bf16[1,24,256]{2,1,0:T(8,128)(2,1)} %param.9) | copy-start | bytes 36868
  73.4 0.8 copy-start.4
  74.2 19.3 %all-to-all-start.3 = ((bf16[32,56,128]{2,1,0:T(8,128)(2,1)}), bf16[32,56,128]{2,1,0:T(8,128)(2,1)S(1)}, u32[]{:S(2)}, u32[]{:S(2)}) async-start(bf16[32,56,128]{2,1,0:T(8,128)(2,1)} %copy-done.4), calls=%async_computation.3 | async-start | bytes 917504 | tf_op jit(solution)/shard_map/all_to_all | solution.py:262
  79.0 15.0 %collective-permute-start = (bf16[24,256]{1,0:T(8,128)(2,1)S(1)}, bf16[24,256]{1,0:T(8,128)(2,1)S(1)}, u32[]{:S(2)}, u32[]{:S(2)}) collective-permute-start(bf16[24,256]{1,0:T(8,128)(2,1)S(1)} %bitcast.42), channel_id=1, source_target_pairs={{0,32},{32,64},{64,96},{96,128},{128,160},{160,192},{192,224},{224... | collective-permute-start | bytes 36872 | tf_op jit(solution)/shard_map/ppermute | solution.py:32
  93.9 4.3 %collective-permute-start.1 = (bf16[24,256]{1,0:T(8,128)(2,1)S(1)}, bf16[24,256]{1,0:T(8,128)(2,1)S(1)}, u32[]{:S(2)}, u32[]{:S(2)}) collective-permute-start(bf16[24,256]{1,0:T(8,128)(2,1)S(1)} %convert_element_type.55), channel_id=1, source_target_pairs={{0,32},{32,64},{64,96},{96,128},{128,160},{160,192},{192,224},{224... | collective-permute-start | bytes 36872 | tf_op jit(solution)/shard_map/ppermute | solution.py:32

commit v2 on v1

v2 whole, which is shorter than its diff:
```python
import math

import jax
import jax.numpy as jnp
from jax import lax
from jax.experimental import pallas as pl
from jax.experimental.pallas import tpu as pltpu
from jax.sharding import PartitionSpec as P

H = 64
KVH = 8
HD = 128
MOST = 2
ROWS = 24
TP = 32
SPAN = 32
QUAD = 4
HEADS_HERE = H // TP
OWN = ROWS * HEADS_HERE
SLOT = 64
PART = 56

EPS = 1e-05
ADAPTER_SCALE = 0.5
NEGATIVE = -1e30
FLOOR = -1e20
FACTOR = 1.0 / math.sqrt(HD)


def passed_along(array, axis, by):
    devices = lax.axis_size(axis)
    return lax.ppermute(array, axis, [(i, (i + by) % devices) for i in range(devices)])


def call(kernel, mebibytes, out_shape, scratch, *arguments):
    vmem, hbm = pl.BlockSpec(memory_space=pltpu.VMEM), pl.BlockSpec(memory_space=pltpu.HBM)
    far = [isinstance(a, Far) for a in arguments]
    values = [pltpu.with_memory_space_constraint(a.array, pltpu.HBM) if f else a for a, f in zip(arguments, far)]
    return pl.pallas_call(
        kernel,
        out_shape=out_shape,
        in_specs=[hbm if f else vmem for f in far],
        out_specs=tuple(hbm if getattr(o, "memory_space", None) == pltpu.HBM else vmem for o in out_shape),
        scratch_shapes=scratch,
        compiler_params=pltpu.CompilerParams(vmem_limit_bytes=mebibytes * 1024 * 1024),
    )(*values)


class Far:
    def __init__(self, array):
        self.array = array


def low_lanes(shape):
    return lax.broadcasted_iota(jnp.int32, shape, len(shape) - 1) < HD // 2


def pack_kernel(base_ref, spread_ref, received_ref, slots_ref):
    received = received_ref[...].reshape(TP * 8, HD)
    tiles = []
    for k in range(3):
        change = jnp.dot(spread_ref[k], received, preferred_element_type=jnp.float32)
        tiles.append(base_ref[:, k * HD : (k + 1) * HD] + change)
    odd = lax.axis_index("tp") % 2 == 1
    turned = [pltpu.roll(tile, HD // 2, 1) for tile in tiles]
    low = low_lanes((ROWS, HD))
    first = jnp.where(odd, jnp.where(low, turned[0], turned[1]), tiles[0])
    second = jnp.where(odd, jnp.where(low, turned[1], turned[2]), tiles[1])
    part = jnp.where(odd, tiles[0], tiles[2])
    turned_part = jnp.where(odd, turned[0], turned[2])
    low = low_lanes((8, HD))
    even_pair = jnp.where(low, part[0:8], turned_part[8:16])
    odd_pair = jnp.where(low, part[8:16], turned_part[0:8])
    pair = jnp.where(odd, odd_pair, even_pair)
    last = jnp.where(odd, turned_part[16:24], part[16:24])
    slot = jnp.concatenate([first, second, pair, last], axis=0).astype(jnp.bfloat16)
    for t in range(TP):
        slots_ref[t] = slot


def attention_kernel(
    slots_ref, used_ref, keys_far, values_far, moved_ref, sent_ref, own_ref, own_value_ref, kept_ref,
    query, fresh, result, levels, biases, keys_ref, values_ref, sent, load_sem, sent_sem, kept_sem,
):
    quads = ROWS // QUAD
    loads = []
    for i, (far, near) in enumerate(((keys_far, keys_ref), (values_far, values_ref))):
        loads.append([])
        for q in range(3):
            part = pl.ds(8 * q, 8)
            loads[i].append(pltpu.make_async_copy(far.at[part], near.at[part], load_sem.at[i, q]))
            loads[i][q].start()
    keep = pltpu.make_async_copy(moved_ref, kept_ref, kept_sem)
    keep.start()
    levels[...] = jnp.full(levels.shape, NEGATIVE, jnp.float32)
    row_lane = lax.broadcasted_iota(jnp.int32, (SPAN, HD), 1) // 2 % QUAD
    position = lax.axis_index("tp") * SPAN + lax.broadcasted_iota(jnp.int32, (SPAN, HD), 0)
    for row in range(ROWS):
        seen = (position < used_ref[row : row + 1, :]) & (row_lane == row % QUAD)
        at = SPAN * (row % QUAD)
        biases[row // QUAD, at : at + SPAN, :] = jnp.where(seen, 0.0, NEGATIVE)
    low = low_lanes((8, HD))

    def put(head, rows):
        if head < H:
            query[head // 2, pl.ds(head % 2, ROWS, stride=2), :] = rows
        else:
            fresh[head - H, pl.ds(0, ROWS, stride=2), :] = rows
            fresh[head - H, pl.ds(1, ROWS, stride=2), :] = rows

    for p in range(TP // 2):
        even = slots_ref[2 * p].astype(jnp.float32)
        odd = slots_ref[2 * p + 1].astype(jnp.float32)
        put(5 * p, even[0:24])
        put(5 * p + 1, even[24:48])
        middle = jnp.where(low, odd[48:56], even[48:56])
        put(
            5 * p + 2,
            jnp.concatenate(
                [
                    jnp.where(low, even[48:56], odd[48:56]),
                    pltpu.roll(middle, HD // 2, 1),
                    jnp.where(low, even[56:64], odd[56:64]),
                ],
                axis=0,
            ),
        )
        put(5 * p + 3, odd[0:24])
        put(5 * p + 4, odd[24:48])

    device = lax.axis_index("tp")
    group = device // (TP // KVH)
    own_level = jnp.sum(query[device] * fresh[group], axis=1, keepdims=True) * FACTOR
    own_ref[...] = jnp.broadcast_to(own_level, (OWN, HD))
    own_value_ref[...] = fresh[KVH + group]

    rows = QUAD * SPAN
    lane = lax.broadcasted_iota(jnp.int32, (HD, HD), 1)
    for load in loads[0]:
        load.wait()
    kept = {}
    for gg in range(2):
        for q in range(quads):
            left = jnp.concatenate([query[16 * gg + j, 8 * q : 8 * q + 8, :] for j in range(16)], axis=0)
            turned = jnp.transpose(left)
            parts = [jnp.where(lane // 32 == i, turned, 0.0).astype(jnp.bfloat16) for i in range(4)]
            right = jnp.concatenate(parts, axis=0)
            keys = keys_ref[QUAD * q : QUAD * (q + 1), :, 512 * gg : 512 * (gg + 1)].reshape(rows, 512)
            scores = jnp.dot(keys, right, preferred_element_type=jnp.float32) * FACTOR + biases[q]
            top = jnp.maximum(jnp.max(scores, axis=0, keepdims=True), FLOOR)
            weights = jnp.exp(scores - top)
            total = jnp.sum(weights, axis=0, keepdims=True)
            some = total > 0.0
            safe = jnp.where(some, total, 1.0)
            levels[gg, q : q + 1, :] = jnp.where(some, top + jnp.log(safe), NEGATIVE)
            kept[gg, q] = jnp.transpose(weights * (1.0 / safe)).astype(jnp.bfloat16)
    for load in loads[1]:
        load.wait()
    eighth = lax.broadcasted_iota(jnp.int32, (8, HD), 1) // 8
    stores = []
    for gg in range(2):
        level = levels[gg]
        high = level.astype(jnp.bfloat16).astype(jnp.float32)
        middle = (level - high).astype(jnp.bfloat16).astype(jnp.float32)
        rest = pltpu.roll(level - high - middle, 16, 1)
        middle = pltpu.roll(middle, 8, 1)
        for q in range(quads):
            for i in range(4):
                g = 4 * gg + i
                part = values_ref[QUAD * q : QUAD * (q + 1), :, g * HD : (g + 1) * HD].reshape(rows, HD)
                mixed = jnp.dot(kept[gg, q][32 * i : 32 * i + 32], part, preferred_element_type=jnp.float32)
                for j in range(4):
                    result[4 * g + j, 8 * q : 8 * q + 8, :] = mixed[8 * j : 8 * j + 8]
        for j in range(16):
            lines = jnp.where(eighth == j, high, jnp.where(eighth == (j + 1) % 16, middle, rest))
            t = 16 * gg + j
            sent[t] = jnp.concatenate([result[t], lines], axis=0).astype(jnp.bfloat16)
        half = pl.ds(16 * gg, 16)
        stores.append(pltpu.make_async_copy(sent.at[half], sent_ref.at[half], sent_sem.at[gg]))
        stores[-1].start()
    for store in stores:
        store.wait()
    keep.wait()


def eighth_lanes():
    return lax.broadcasted_iota(jnp.int32, (8, HD), 1) < 8


def combine_kernel(arrived_ref, own_ref, own_value_ref, context_ref):
    quads = ROWS // QUAD
    turn = (HD - 8 * (lax.axis_index("tp") % 16)) % HD
    eye = lax.broadcasted_iota(jnp.int32, (8, HD), 0) == lax.broadcasted_iota(jnp.int32, (8, HD), 1)
    own = [
        jnp.sum(jnp.where(eye, own_ref[8 * q : 8 * q + 8, :], 0.0), axis=0, keepdims=True) for q in range(quads)
    ]
    own = jnp.concatenate(own + [jnp.zeros((8 - quads, HD), jnp.float32)], axis=0)
    levels = []
    for t in range(TP):
        terms = arrived_ref[t].astype(jnp.float32)[OWN:PART]
        levels.append(terms + pltpu.roll(terms, HD - 8, 1) + pltpu.roll(terms, HD - 16, 1))
    levels = [jnp.where(eighth_lanes(), pltpu.roll(level, turn, 1), 0.0) for level in levels]
    highest = own
    for level in levels:
        highest = jnp.maximum(highest, level)
    shares = [jnp.exp(level - highest) for level in levels]
    own = jnp.exp(own - highest)
    whole = own
    for share in shares:
        whole = whole + share
    scale = 1.0 / whole
    shares = [share * scale for share in shares]
    columns = [jnp.transpose(jnp.concatenate(shares[16 * i : 16 * i + 16], axis=0)) for i in range(2)]
    own = jnp.transpose(jnp.concatenate([own * scale] + [jnp.zeros((HD - 8, HD), jnp.float32)], axis=0))
    totals = [own[0:8, q : q + 1] * own_value_ref[8 * q : 8 * q + 8, :] for q in range(quads)]
    for t in range(TP):
        rows = arrived_ref[t].astype(jnp.float32)
        for q in range(quads):
            at = 8 * (t % 16) + q
            totals[q] = totals[q] + columns[t // 16][0:8, at : at + 1] * rows[8 * q : 8 * q + 8]
    context_ref[...] = jnp.concatenate(totals, axis=0)


def on_device(
    hidden,
    attention_norm_scale,
    joined_projection_weight,
    adapter_down_weight,
    adapter_up_weight,
    cached_key_rows,
    cached_value_rows,
    row_adapter_index,
    lengths,
):
    width = lax.axis_size("tp")
    device = lax.axis_index("tp")
    rows_here = hidden[0]
    batch, features = rows_here.shape
    moved_rows = passed_along(rows_here, "section", 1)

    chosen = row_adapter_index[0, :, 0]
    same = chosen[:, None] == chosen[None, :]
    earlier = jnp.arange(batch)[None, :] < jnp.arange(batch)[:, None]
    place = jnp.sum(same & earlier, axis=1)
    mine = (chosen[None, :] == device) & (place[None, :] == jnp.arange(MOST)[:, None])
    slot_of_row = chosen * 8 + place * 3
    lines = slot_of_row[None, :, None] + jnp.arange(3)[:, None, None]
    spread = (lines == jnp.arange(width * 8)[None, None, :]).astype(jnp.bfloat16)

    cache = cached_key_rows.shape[1:]
    copies = jnp.broadcast_to(rows_here[None], (width, batch, features))
    pieces = lax.all_to_all(copies, "tp", 0, 0)
    gathered = pieces.transpose(1, 0, 2).reshape(batch, width * features)
    wide = gathered.astype(jnp.float32)
    inverse = lax.rsqrt(jnp.mean(wide * wide, axis=-1, keepdims=True) + EPS)
    normed = (wide * inverse * attention_norm_scale).astype(jnp.bfloat16)
    shrunk = jnp.dot(normed, adapter_down_weight[0, 0], preferred_element_type=jnp.float32)
    picked = jnp.dot(
        mine.astype(jnp.bfloat16), shrunk.astype(jnp.bfloat16), preferred_element_type=jnp.float32
    ).astype(jnp.bfloat16)
    update = jnp.dot(picked, adapter_up_weight[0, 0], preferred_element_type=jnp.float32)
    columns = update.shape[1] // width
    update = (update * ADAPTER_SCALE).astype(jnp.bfloat16).reshape(MOST, width, columns)
    update = jnp.pad(update.transpose(1, 0, 2), ((0, 0), (0, 0), (0, 3 * HD - columns)))
    update = jnp.pad(update.reshape(width, 3 * MOST, HD), ((0, 0), (0, 8 - 3 * MOST), (0, 0)))
    received = lax.all_to_all(update, "tp", 0, 0)
    base = jnp.dot(normed, joined_projection_weight[0], preferred_element_type=jnp.float32)
    base = jnp.pad(base, ((0, 0), (0, 3 * HD - base.shape[1])))
    (slots,) = call(
        pack_kernel,
        4,
        (jax.ShapeDtypeStruct((TP, SLOT, HD), jnp.bfloat16),),
        [],
        base,
        spread,
        received,
    )
    joined = lax.all_to_all(slots, "tp", 0, 0)

    sent, own, own_value, moved_rows = call(
        attention_kernel,
        12,
        (
            pltpu.HBM((TP, PART, HD), jnp.bfloat16),
            jax.ShapeDtypeStruct((OWN, HD), jnp.float32),
            jax.ShapeDtypeStruct((OWN, HD), jnp.float32),
            pltpu.HBM((batch, features), jnp.bfloat16),
        ),
        [
            pltpu.VMEM((TP, OWN, HD), jnp.float32),
            pltpu.VMEM((2 * KVH, OWN, HD), jnp.float32),
            pltpu.VMEM((TP, OWN, HD), jnp.float32),
            pltpu.VMEM((2, 8, HD), jnp.float32),
            pltpu.VMEM((batch // QUAD, QUAD * SPAN, HD), jnp.float32),
            pltpu.VMEM(cache, jnp.bfloat16),
            pltpu.VMEM(cache, jnp.bfloat16),
            pltpu.VMEM((TP, PART, HD), jnp.bfloat16),
            pltpu.SemaphoreType.DMA((2, 3)),
            pltpu.SemaphoreType.DMA((2,)),
            pltpu.SemaphoreType.DMA,
        ],
        joined,
        jnp.broadcast_to(lengths[0][:, None], (batch, HD)),
        Far(cached_key_rows[0]),
        Far(cached_value_rows[0]),
        moved_rows,
    )
    arrived = lax.all_to_all(sent, "tp", 0, 0)
    (context,) = call(
        combine_kernel,
        4,
        (jax.ShapeDtypeStruct((OWN, HD), jnp.float32),),
        [],
        arrived,
        own,
        own_value,
    )
    context = context.reshape(batch, HEADS_HERE * HD).astype(jnp.bfloat16)
    moved_context = passed_along(context, "section", 1)
    return (moved_rows[None], moved_context[None])


def solution(mesh):
    return jax.shard_map(
        on_device,
        mesh=mesh,
        in_specs=(
            P("section", None, "tp"),
            P(),
            P("section", None, "tp"),
            P("section", "tp", None, None),
            P("section", "tp", None, None),
            P("section", None, "tp", None),
            P("section", None, "tp", None),
            P("section", None, None),
            P("section", None),
        ),
        out_specs=(P("section", None, "tp"), P("section", None, "tp")),
        check_vma=False,
    )
```

time: 100 us -> 96.1 us (0.961)
  blocking collectives: 0 us -> 19.3 us
  local copies, waits for them, and re-layouts: 14.7 us -> 4.01 us
  waiting for transfers between devices: 44.2 us -> 37.6 us
  starting transfers between devices: 25.7 us -> 20.9 us
    all_to_all x0 -> x1, blocking collectives: none -> 19.3 us  [on_device(): arrived = lax.all_to_all(sent, 'tp', 0, 0)]
    all_to_all x2 -> x1, waiting for transfers between devices: 26.1 us -> 11.8 us  [on_device(): pieces = lax.all_to_all(copies, 'tp', 0, 0)]
    reshape x2 -> x0, local copies, waits for them, and re-layouts: 4.87 us -> none  [on_device(): bias = bias.reshape(batch // QUAD, QUAD * span, HD)]
    all_to_all x2 -> x1, starting transfers between devices: 16.2 us -> 11.4 us  [on_device(): pieces = lax.all_to_all(copies, 'tp', 0, 0)]
    ppermute x2, waiting for transfers between devices: 4.31 us -> 8.63 us  [passed_along(): lax.ppermute(array, axis, [(i, (i + by) % devices) for i in range(devices)])]
    unnamed x19 -> x9, local copies, waits for them, and re-layouts: 4.91 us -> 0.63 us
    all_to_all x1, waiting for transfers between devices: 8.69 us -> 12.2 us  [on_device(): joined = lax.all_to_all(slots, 'tp', 0, 0)]
    broadcast_in_dim x2, local copies, waits for them, and re-layouts: 3.15 us -> 1.7 us  [the longest x1 1.63 us: on_device(): copies = jnp.broadcast_to(rows_here[None], (width, batch, features))]
  transfers between devices with their start and end apart: 6 -> 5, of which waited for: 5 -> 5; matrix products, arithmetic and copies ran while one was open for 15% -> 7% of each run, Pallas kernels for 1% -> 0%
where the time goes in v2:
time: 96.1 us; the launch traced here: 95.5 us
  waiting for transfers between devices  37.6 us (39%)
  starting transfers between devices  20.9 us (22%)
  blocking collectives  19.3 us (20%)
  Pallas kernels  5.35 us (6%)
  matrix products  4.79 us (5%)
  local copies, waits for them, and re-layouts  4.01 us (4%)
  other arithmetic  2.72 us (3%)
    all_to_all x1, blocking collectives, on_device(): arrived = lax.all_to_all(sent, 'tp', 0, 0)  19.3 us
    all_to_all x1, waiting for transfers between devices, on_device(): joined = lax.all_to_all(slots, 'tp', 0, 0)  12.2 us
    all_to_all x1, waiting for transfers between devices, on_device(): pieces = lax.all_to_all(copies, 'tp', 0, 0)  11.8 us
    all_to_all x1, starting transfers between devices, on_device(): pieces = lax.all_to_all(copies, 'tp', 0, 0)  11.4 us
    ppermute x2, waiting for transfers between devices, passed_along(): lax.ppermute(array, axis, [(i, (i + by) % devices) for i in range(devices)])  8.63 us
    pallas_call x3, Pallas kernels, call(): pl.pallas_call(kernel, out_shape=out_shape, in_specs=[hbm if f else vmem...  5.35 us
    all_to_all x1, waiting for transfers between devices, on_device(): received = lax.all_to_all(update, 'tp', 0, 0)  5.07 us
    all_to_all x1, starting transfers between devices, on_device(): received = lax.all_to_all(update, 'tp', 0, 0)  4.78 us
  transfers between devices with their start and end apart: 5, of which 5 were waited for; matrix products, arithmetic and copies ran while one was open for 7% of the time, Pallas kernels for 0%

profile of v2, /device:TPU:32, one launch (start us, length us, event | category | flops | bytes accessed | tf_op | source)
XLA Modules:
  0.0 95.5 jit_solution(12123600178553743951)
XLA Ops:
  0.6 0.0 copy-start
  0.6 0.0 copy-start.1
  0.7 1.6 %broadcast_in_dim.13 = bf16[32,24,256]{2,1,0:T(8,128)(2,1)} broadcast(bf16[24,256]{1,0:T(8,128)(2,1)} %bitcast.39), dimensions={1,2} | broadcast | bytes 405504 | tf_op jit(solution)/shard_map/broadcast_in_dim | solution.py:251
  2.3 11.4 %all-to-all-start = ((bf16[32,24,256]{2,1,0:T(8,128)(2,1)}), bf16[32,24,256]{2,1,0:T(8,128)(2,1)S(1)}, u32[]{:S(2)}, u32[]{:S(2)}) async-start(bf16[32,24,256]{2,1,0:T(8,128)(2,1)} %broadcast_in_dim.13), calls=%async_computation | async-start | bytes 786432 | tf_op jit(solution)/shard_map/all_to_all | solution.py:252
  13.7 0.8 mul.55
  14.4 0.7 broadcast_compare_fusion
  15.1 0.9 convert_reduce_fusion
  16.0 0.7 fusion.18
  16.7 0.1 fusion.12.spread_ref
  16.8 11.8 %all-to-all-done = bf16[32,24,256]{2,1,0:T(8,128)(2,1)S(1)} async-done(((bf16[32,24,256]{2,1,0:T(8,128)(2,1)}), bf16[32,24,256]{2,1,0:T(8,128)(2,1)S(1)}, u32[]{:S(2)}, u32[]{:S(2)}) %all-to-all-start) | async-done | bytes 393248 | tf_op jit(solution)/shard_map/all_to_all | solution.py:252
  28.5 0.2 fusion.8
  28.8 0.2 fusion.11
  29.0 0.0 copy-done.1
  29.0 0.5 fusion.5
  29.5 0.0 copy-done
  29.5 0.3 fusion
  29.8 0.1 reshape.87
  30.1 0.6 pad.14
  30.7 4.8 %all-to-all-start.1 = ((bf16[32,8,128]{2,1,0:T(8,128)(2,1)}), bf16[32,8,128]{2,1,0:T(8,128)(2,1)S(1)}, u32[]{:S(2)}, u32[]{:S(2)}) async-start(bf16[32,8,128]{2,1,0:T(8,128)(2,1)} %pad.14), calls=%async_computation.1 | async-start | bytes 131072 | tf_op jit(solution)/shard_map/all_to_all | solution.py:266
  35.5 4.0 %fusion.1 = f32[24,320]{1,0:T(8,128)S(1)} fusion(bf16[24,8192]{1,0:T(8,128)(2,1)S(1)} %bitcast.35, bf16[1,8192,320]{1,2,0:T(8,128)(2,1)} %param.11), kind=kOutput, calls=%fused_computation.2 | convolution fusion | flops 125829120 | bytes 5666816 | tf_op jit(solution)/shard_map/dot_general | solution.py:267
  39.5 0.0 copy-start.2
  39.5 0.0 copy-start.3
  39.5 5.1 %all-to-all-done.1.received_ref = bf16[32,8,128]{2,1,0:T(8,128)(2,1)S(1)} async-done(((bf16[32,8,128]{2,1,0:T(8,128)(2,1)}), bf16[32,8,128]{2,1,0:T(8,128)(2,1)S(1)}, u32[]{:S(2)}, u32[]{:S(2)}) %all-to-all-start.1) | async-done | bytes 65568 | tf_op jit(solution)/shard_map/all_to_all | solution.py:266
  44.6 1.1 %shard_map.104 = bf16[32,64,128]{2,1,0:T(8,128)(2,1)} custom-call(f32[24,384]{1,0:T(8,128)S(1)} %pad.12.base_ref, bf16[3,24,256]{2,1,0:T(8,128)(2,1)S(1)} %fusion.12.spread_ref, bf16[32,8,128]{2,1,0:T(8,128)(2,1)S(1)} %all-to-all-done.1.received_ref), custom_call_target="tpu_custom_call" | custom-call | tf_op jit(solution)/shard_map/pallas_call | solution.py:39
  45.6 4.7 %all-to-all-start.2 = ((bf16[32,64,128]{2,1,0:T(8,128)(2,1)}), bf16[32,64,128]{2,1,0:T(8,128)(2,1)S(1)}, u32[]{:S(2)}, u32[]{:S(2)}) async-start(bf16[32,64,128]{2,1,0:T(8,128)(2,1)} %shard_map.104), calls=%async_computation.2 | async-start | bytes 1048576 | tf_op jit(solution)/shard_map/all_to_all | solution.py:278
  50.4 0.0 copy-done.2
  50.4 0.0 collective-permute-start
  50.4 4.3 %collective-permute-done.moved_ref = bf16[24,256]{1,0:T(8,128)(2,1)S(1)} collective-permute-done((bf16[24,256]{1,0:T(8,128)(2,1)S(1)}, bf16[24,256]{1,0:T(8,128)(2,1)S(1)}, u32[]{:S(2)}, u32[]{:S(2)}) %collective-permute-start) | collective-permute-done | bytes 12320 | tf_op jit(solution)/shard_map/ppermute | solution.py:32
  54.7 12.2 %all-to-all-done.2.slots_ref = bf16[32,64,128]{2,1,0:T(8,128)(2,1)S(1)} async-done(((bf16[32,64,128]{2,1,0:T(8,128)(2,1)}), bf16[32,64,128]{2,1,0:T(8,128)(2,1)S(1)}, u32[]{:S(2)}, u32[]{:S(2)}) %all-to-all-start.2) | async-done | bytes 524320 | tf_op jit(solution)/shard_map/all_to_all | solution.py:278
  66.9 0.0 copy-done.3
  66.9 0.1 broadcast_in_dim.15.used_ref
  67.0 3.6 %shard_map.105 = (bf16[32,56,128]{2,1,0:T(8,128)(2,1)}, f32[48,128]{1,0:T(8,128)S(1)}, f32[48,128]{1,0:T(8,128)S(1)}, bf16[24,256]{1,0:T(8,128)(2,1)}) custom-call(bf16[32,64,128]{2,1,0:T(8,128)(2,1)S(1)} %all-to-all-done.2.slots_ref, s32[24,128]{1,0:T(8,128)S(1)} %broadcast_in_dim.15.used_ref, bf16[24,32,1024]{2,1,0:T(8,128)(2,1)} %bitcast.36, ...), custom_call_target="tpu_custom_call" | custom-call | tf_op jit(solution)/shard_map/pallas_call | solution.py:39
  70.6 19.3 %all_to_all.20.arrived_ref = bf16[32,56,128]{2,1,0:T(8,128)(2,1)S(1)} all-to-all(bf16[32,56,128]{2,1,0:T(8,128)(2,1)} %get-tuple-element.7), channel_id=1, replica_groups=mesh['section'=8,'tp'=32] {'tp'}, dimensions={0} | all-to-all | bytes 917504 | tf_op jit(solution)/shard_map/all_to_all | solution.py:308
  89.8 0.7 shard_map.106
  90.6 0.0 collective-permute-start.1
  90.6 4.3 %collective-permute-done.1 = bf16[24,256]{1,0:T(8,128)(2,1)S(1)} collective-permute-done((bf16[24,256]{1,0:T(8,128)(2,1)S(1)}, bf16[24,256]{1,0:T(8,128)(2,1)S(1)}, u32[]{:S(2)}, u32[]{:S(2)}) %collective-permute-start.1) | collective-permute-done | bytes 12320 | tf_op jit(solution)/shard_map/ppermute | solution.py:32
  94.9 0.6 copy.21
  (9 shorter events, 0.2 us)
Async XLA Ops:
  0.6 28.9 %copy-start = (bf16[1,1,64,10240]{3,2,1,0:T(8,128)(2,1)S(1)}, bf16[1,1,64,10240]{3,2,1,0:T(8,128)(2,1)}, u32[]{:S(2)}) copy-start(bf16[1,1,64,10240]{3,2,1,0:T(8,128)(2,1)} %param.13) | copy-start | bytes 3932164
  0.6 28.3 %copy-start.1 = (bf16[1,1,8192,64]{2,3,1,0:T(8,128)(2,1)S(1)}, bf16[1,1,8192,64]{2,3,1,0:T(8,128)(2,1)}, u32[]{:S(2)}) copy-start(bf16[1,1,8192,64]{2,3,1,0:T(8,128)(2,1)} %param.12) | copy-start | bytes 3145732
  2.3 26.2 %all-to-all-start = ((bf16[32,24,256]{2,1,0:T(8,128)(2,1)}), bf16[32,24,256]{2,1,0:T(8,128)(2,1)S(1)}, u32[]{:S(2)}, u32[]{:S(2)}) async-start(bf16[32,24,256]{2,1,0:T(8,128)(2,1)} %broadcast_in_dim.13), calls=%async_computation | async-start | bytes 786432 | tf_op jit(solution)/shard_map/all_to_all | solution.py:252
  30.7 13.9 %all-to-all-start.1 = ((bf16[32,8,128]{2,1,0:T(8,128)(2,1)}), bf16[32,8,128]{2,1,0:T(8,128)(2,1)S(1)}, u32[]{:S(2)}, u32[]{:S(2)}) async-start(bf16[32,8,128]{2,1,0:T(8,128)(2,1)} %pad.14), calls=%async_computation.1 | async-start | bytes 131072 | tf_op jit(solution)/shard_map/all_to_all | solution.py:266
  39.5 10.9 %copy-start.2 = (bf16[1,24,256]{2,1,0:T(8,128)(2,1)S(1)}, bf16[1,24,256]{2,1,0:T(8,128)(2,1)}, u32[]{:S(2)}) copy-start(bf16[1,24,256]{2,1,0:T(8,128)(2,1)} %param.9) | copy-start | bytes 36868
  39.5 27.4 %copy-start.3 = (s32[1,24]{1,0:T(1,128)S(1)}, s32[1,24]{1,0:T(1,128)}, u32[]{:S(2)}) copy-start(s32[1,24]{1,0:T(1,128)} %param.17) | copy-start | bytes 292
  45.6 21.3 %all-to-all-start.2 = ((bf16[32,64,128]{2,1,0:T(8,128)(2,1)}), bf16[32,64,128]{2,1,0:T(8,128)(2,1)S(1)}, u32[]{:S(2)}, u32[]{:S(2)}) async-start(bf16[32,64,128]{2,1,0:T(8,128)(2,1)} %shard_map.104), calls=%async_computation.2 | async-start | bytes 1048576 | tf_op jit(solution)/shard_map/all_to_all | solution.py:278
  50.4 4.3 %collective-permute-start = (bf16[24,256]{1,0:T(8,128)(2,1)S(1)}, bf16[24,256]{1,0:T(8,128)(2,1)S(1)}, u32[]{:S(2)}, u32[]{:S(2)}) collective-permute-start(bf16[24,256]{1,0:T(8,128)(2,1)S(1)} %bitcast.40), channel_id=1, source_target_pairs={{0,32},{32,64},{64,96},{96,128},{128,160},{160,192},{192,224},{224... | collective-permute-start | bytes 36872 | tf_op jit(solution)/shard_map/ppermute | solution.py:32
  90.6 4.3 %collective-permute-start.1 = (bf16[24,256]{1,0:T(8,128)(2,1)S(1)}, bf16[24,256]{1,0:T(8,128)(2,1)S(1)}, u32[]{:S(2)}, u32[]{:S(2)}) collective-permute-start(bf16[24,256]{1,0:T(8,128)(2,1)S(1)} %convert_element_type.55), channel_id=1, source_target_pairs={{0,32},{32,64},{64,96},{96,128},{128,160},{160,192},{192,224},{224... | collective-permute-start | bytes 36872 | tf_op jit(solution)/shard_map/ppermute | solution.py:32

commit v3 on v2

v3 whole, which is shorter than its diff:
```python
import math

import jax
import jax.numpy as jnp
from jax import lax
from jax.experimental import pallas as pl
from jax.experimental.pallas import tpu as pltpu
from jax.sharding import PartitionSpec as P

H = 64
KVH = 8
HD = 128
MOST = 2
ROWS = 24
TP = 32
SPAN = 32
QUAD = 4
NEAR = 8
SHARE = ROWS // 2
GIVEN = SHARE // 2
QUADS = SHARE // QUAD
HEADS_HERE = H // TP
LINES = SHARE * HEADS_HERE
SLOT = 32
PART = LINES + 8

EPS = 1e-05
ADAPTER_SCALE = 0.5
NEGATIVE = -1e30
FLOOR = -1e20
FACTOR = 1.0 / math.sqrt(HD)


def passed_along(array, axis, by):
    devices = lax.axis_size(axis)
    return lax.ppermute(array, axis, [(i, (i + by) % devices) for i in range(devices)])


def call(kernel, mebibytes, out_shape, scratch, *arguments):
    vmem, hbm = pl.BlockSpec(memory_space=pltpu.VMEM), pl.BlockSpec(memory_space=pltpu.HBM)
    far = [isinstance(a, Far) for a in arguments]
    values = [pltpu.with_memory_space_constraint(a.array, pltpu.HBM) if f else a for a, f in zip(arguments, far)]
    return pl.pallas_call(
        kernel,
        out_shape=out_shape,
        in_specs=[hbm if f else vmem for f in far],
        out_specs=tuple(hbm if getattr(o, "memory_space", None) == pltpu.HBM else vmem for o in out_shape),
        scratch_shapes=scratch,
        compiler_params=pltpu.CompilerParams(vmem_limit_bytes=mebibytes * 1024 * 1024),
    )(*values)


class Far:
    def __init__(self, array):
        self.array = array


def low_lanes(shape):
    return lax.broadcasted_iota(jnp.int32, shape, len(shape) - 1) < HD // 2


def pack_kernel(base_ref, spread_ref, received_ref, *rest):
    slots_ref = rest[-1]
    received = received_ref[...].reshape(TP * 8, HD)
    tiles = []
    for k in range(3):
        change = jnp.dot(spread_ref[k], received, preferred_element_type=jnp.float32)
        tiles.append(base_ref[:, k * HD : (k + 1) * HD] + change)
    odd = lax.axis_index("tp") % 2 == 1
    turned = [pltpu.roll(tile, HD // 2, 1) for tile in tiles]
    low = low_lanes((ROWS, HD))
    first = jnp.where(odd, jnp.where(low, turned[0], turned[1]), tiles[0])
    second = jnp.where(odd, jnp.where(low, turned[1], turned[2]), tiles[1])
    part = jnp.where(odd, tiles[0], tiles[2])
    turned_part = jnp.where(odd, turned[0], turned[2])
    low = low_lanes((8, HD))
    upper = lax.broadcasted_iota(jnp.int32, (8, HD), 0) < 4
    slots = []
    for side in range(2):
        main = slice(16 * side, 16 * side + 8)
        firsts, seconds, parts, turned_parts = (v[8:16] for v in (first, second, part, turned_part))
        if side == 0:
            seconds = pltpu.roll(seconds, 4, 0)
        else:
            firsts, parts, turned_parts = (pltpu.roll(v, 4, 0) for v in (firsts, parts, turned_parts))
        left = jnp.where(upper, firsts, seconds)
        even_half = jnp.where(low, part[main], turned_parts)
        odd_half = jnp.where(low, parts, turned_part[main])
        half = jnp.where(odd, odd_half, even_half)
        slots.append(jnp.concatenate([first[main], second[main], left, half], axis=0).astype(jnp.bfloat16))
    for t in range(TP):
        slots_ref[t] = slots[t // NEAR % 2]


def attention_kernel(
    slots_ref, limit_ref, keys_far, values_far, keys_a, keys_b, values_a, values_b, moved_ref, sent_ref, kept_ref,
    query, fresh, result, levels, added, biases, keys_ref, values_ref, sent, load_sem, given_sem, sent_sem, kept_sem,
):
    device = lax.axis_index("tp")
    side = device // NEAR % 2
    caches = ((keys_far, keys_a, keys_b, keys_ref), (values_far, values_a, values_b, values_ref))

    def own_load(i, q):
        start = SHARE * side + QUAD * lax.rem(q + side, QUADS)
        far, near = caches[i][0], caches[i][3]
        return pltpu.make_async_copy(far.at[pl.ds(start, QUAD)], near.at[q, 0], load_sem.at[i, q])

    def given_load(i, p, on_side):
        row = (2 * p + QUAD * on_side) % SHARE
        far, near = caches[i][1 + row // GIVEN], caches[i][3]
        return pltpu.make_async_copy(
            far.at[pl.ds(row % GIVEN, 2)], near.at[p // 2, 1, pl.ds(2 * (p % 2), 2)], given_sem.at[i, p]
        )

    for i in range(2):
        for q in range(QUADS):
            own_load(i, q).start()
        for on_side in range(2):

            @pl.when(side == on_side)
            def _():
                for p in range(2 * QUADS):
                    given_load(i, p, on_side).start()

    keep = pltpu.make_async_copy(moved_ref, kept_ref, kept_sem)
    keep.start()
    levels[...] = jnp.full(levels.shape, NEGATIVE, jnp.float32)
    added[...] = jnp.zeros(added.shape, jnp.float32)
    row_lane = lax.broadcasted_iota(jnp.int32, (SPAN, HD), 1) // 2 % QUAD
    position = lax.broadcasted_iota(jnp.int32, (SPAN, HD), 0)
    for block in range(2):
        for row in range(SHARE):
            at = block * SHARE + row
            seen = (position < limit_ref[at : at + 1, :]) & (row_lane == row % QUAD)
            to = SPAN * (QUAD * block + row % QUAD)
            biases[row // QUAD, to : to + SPAN, :] = jnp.where(seen, 0.0, NEGATIVE)
    low = low_lanes((8, HD))

    def put(head, main, left):
        def store(ref, at, side):
            ref[at, pl.ds(side, 8, stride=2), :] = main
            ref[at, pl.ds(16 + side, 4, stride=2), :] = left[0:4]

        if head < H:
            store(query, head // 2, head % 2)
        else:
            store(fresh, head - H, 0)
            store(fresh, head - H, 1)

    for p in range(TP // 2):
        even = slots_ref[2 * p].astype(jnp.float32)
        odd = slots_ref[2 * p + 1].astype(jnp.float32)
        for head, tile in ((5 * p, even), (5 * p + 3, odd)):
            put(head, tile[0:8], tile[16:24])
            put(head + 1, tile[8:16], pltpu.roll(tile[16:24], 4, 0))
        left = pltpu.roll(jnp.where(low, odd[24:32], even[24:32]), HD // 2, 1)
        put(5 * p + 2, jnp.where(low, even[24:32], odd[24:32]), left)

    eighth = lax.broadcasted_iota(jnp.int32, (8, HD), 1) // 8
    eye = lax.broadcasted_iota(jnp.int32, (8, HD), 0) == lax.broadcasted_iota(jnp.int32, (8, HD), 1)
    own_devices = (device, device + NEAR - 2 * NEAR * side)
    own_lines = jnp.full((8, HD), NEGATIVE, jnp.float32)
    for at in own_devices:
        own = query[at] * fresh[at // (TP // KVH)]
        level = jnp.sum(own, axis=1, keepdims=True) * FACTOR
        lines = [
            jnp.sum(jnp.where(eye, level[8 * q : 8 * q + 8], 0.0), axis=0, keepdims=True) for q in range(QUADS)
        ]
        lines = jnp.concatenate(lines + [jnp.zeros((8 - QUADS, HD), jnp.float32)], axis=0)
        own_lines = jnp.where(eighth == at % 16, pltpu.roll(lines, 8 * (at % 16), 1), own_lines)

    rows = 2 * QUAD * SPAN
    lane = lax.broadcasted_iota(jnp.int32, (HD, HD), 1)
    for q in range(QUADS):
        own_load(0, q).wait()
    for p in range(2 * QUADS):
        given_load(0, p, 0).wait()
    kept = {}
    for gg in range(2):
        own_here = jnp.where(device // 16 == gg, own_lines, NEGATIVE)
        for q in range(QUADS):
            left = jnp.concatenate([query[16 * gg + j, 8 * q : 8 * q + 8, :] for j in range(16)], axis=0)
            turned = jnp.transpose(left)
            parts = [jnp.where(lane // 32 == i, turned, 0.0).astype(jnp.bfloat16) for i in range(4)]
            right = jnp.concatenate(parts, axis=0)
            keys = keys_ref[q, :, :, :, 512 * gg : 512 * (gg + 1)].reshape(rows, 512)
            scores = jnp.dot(keys, right, preferred_element_type=jnp.float32) * FACTOR + biases[q]
            own = own_here[q : q + 1, :]
            top = jnp.maximum(jnp.maximum(jnp.max(scores, axis=0, keepdims=True), own), FLOOR)
            weights = jnp.exp(scores - top)
            own = jnp.exp(own - top)
            total = jnp.sum(weights, axis=0, keepdims=True) + own
            some = total > 0.0
            safe = jnp.where(some, total, 1.0)
            levels[gg, q : q + 1, :] = jnp.where(some, top + jnp.log(safe), NEGATIVE)
            scale = 1.0 / safe
            added[q : q + 1, :] = added[q : q + 1, :] + own * scale
            kept[gg, q] = jnp.transpose(weights * scale).astype(jnp.bfloat16)
    own_terms = []
    for at in own_devices:
        lines = pltpu.roll(added[...], lax.rem(HD - 8 * (at % 16), HD), 1)
        columns = jnp.transpose(jnp.concatenate([lines, jnp.zeros((HD - 8, HD), jnp.float32)], axis=0))
        value = fresh[KVH + at // (TP // KVH)]
        terms = [columns[0:8, q : q + 1] * value[8 * q : 8 * q + 8] for q in range(QUADS)]
        own_terms.append(jnp.concatenate(terms, axis=0))
    for q in range(QUADS):
        own_load(1, q).wait()
    for p in range(2 * QUADS):
        given_load(1, p, 0).wait()
    stores = []
    for gg in range(2):
        level = levels[gg]
        high = level.astype(jnp.bfloat16).astype(jnp.float32)
        middle = (level - high).astype(jnp.bfloat16).astype(jnp.float32)
        rest = pltpu.roll(level - high - middle, 16, 1)
        middle = pltpu.roll(middle, 8, 1)
        for q in range(QUADS):
            for i in range(4):
                g = 4 * gg + i
                part = values_ref[q, :, :, :, g * HD : (g + 1) * HD].reshape(rows, HD)
                mixed = jnp.dot(kept[gg, q][32 * i : 32 * i + 32], part, preferred_element_type=jnp.float32)
                for j in range(4):
                    result[4 * g + j, 8 * q : 8 * q + 8, :] = mixed[8 * j : 8 * j + 8]
        for j in range(16):
            lines = jnp.where(eighth == j, high, jnp.where(eighth == (j + 1) % 16, middle, rest))
            t = 16 * gg + j
            whole = result[t]
            for at, terms in zip(own_devices, own_terms):
                whole = whole + jnp.where(at == t, terms, 0.0)
            sent[t] = jnp.concatenate([whole, lines], axis=0).astype(jnp.bfloat16)
        half = pl.ds(16 * gg, 16)
        stores.append(pltpu.make_async_copy(sent.at[half], sent_ref.at[half], sent_sem.at[gg]))
        stores[-1].start()
    for store in stores:
        store.wait()
    keep.wait()


def combine_kernel(arrived_ref, context_ref):
    turn = lax.rem(HD - 8 * (lax.axis_index("tp") % 16), HD)
    eight = lax.broadcasted_iota(jnp.int32, (8, HD), 1) < 8
    pieces = []
    for side in range(2):
        sources = [t for t in range(TP) if t // NEAR % 2 == side]
        levels = []
        for t in sources:
            terms = pltpu.roll(arrived_ref[t].astype(jnp.float32)[LINES:PART], turn, 1)
            terms = terms + pltpu.roll(terms, HD - 8, 1) + pltpu.roll(terms, HD - 16, 1)
            levels.append(jnp.where(eight, terms, 0.0))
        highest = levels[0]
        for level in levels[1:]:
            highest = jnp.maximum(highest, level)
        shares = [jnp.exp(level - highest) for level in levels]
        whole = shares[0]
        for share in shares[1:]:
            whole = whole + share
        scale = 1.0 / whole
        columns = jnp.transpose(jnp.concatenate([share * scale for share in shares], axis=0))
        totals = [jnp.zeros((8, HD), jnp.float32)] * QUADS
        for i, t in enumerate(sources):
            rows = arrived_ref[t].astype(jnp.float32)
            for q in range(QUADS):
                at = 8 * i + q
                totals[q] = totals[q] + columns[0:8, at : at + 1] * rows[8 * q : 8 * q + 8]
        pieces += totals if side == 0 else [totals[2], totals[0], totals[1]]
    context_ref[...] = jnp.concatenate(pieces, axis=0)


def on_device(
    hidden,
    attention_norm_scale,
    joined_projection_weight,
    adapter_down_weight,
    adapter_up_weight,
    cached_key_rows,
    cached_value_rows,
    row_adapter_index,
    lengths,
):
    width = lax.axis_size("tp")
    device = lax.axis_index("tp")
    rows_here = hidden[0]
    batch, features = rows_here.shape
    moved_rows = passed_along(rows_here, "section", 1)

    chosen = row_adapter_index[0, :, 0]
    same = chosen[:, None] == chosen[None, :]
    earlier = jnp.arange(batch)[None, :] < jnp.arange(batch)[:, None]
    place = jnp.sum(same & earlier, axis=1)
    mine = (chosen[None, :] == device) & (place[None, :] == jnp.arange(MOST)[:, None])
    slot_of_row = chosen * 8 + place * 3
    lines = slot_of_row[None, :, None] + jnp.arange(3)[:, None, None]
    spread = (lines == jnp.arange(width * 8)[None, None, :]).astype(jnp.bfloat16)

    side = device // NEAR % 2
    wide = width // NEAR
    at = [(y, z) for y in range(wide) for z in range(NEAR)]
    meetings = ([(y * NEAR + z, (y ^ 1) * NEAR + z) for y, z in at], [(y * NEAR + z, (wide - 1 - y) * NEAR + z) for y, z in at])
    given = []
    for cached in (cached_key_rows[0], cached_value_rows[0]):
        for i, pairs in enumerate(meetings):
            part = lax.dynamic_slice_in_dim(cached, SHARE * (1 - side) + GIVEN * i, GIVEN, 0)
            given.append(lax.ppermute(part, "tp", pairs))
    span = cached_key_rows.shape[2]
    used = lengths[0]
    turned = jnp.concatenate([used[SHARE + QUAD :], used[SHARE : SHARE + QUAD]])
    used = jnp.where(side == 0, used[:SHARE], turned)
    row = (jnp.arange(SHARE) + QUAD * side) % SHARE
    y, z = device // NEAR, device % NEAR
    giver = jnp.where(row < GIVEN, y ^ 1, wide - 1 - y) * NEAR + z
    limits = jnp.concatenate([used - span * device, used - span * giver])
    limits = jnp.broadcast_to(limits[:, None], (2 * SHARE, HD))
    near_cache = (QUADS, 2, QUAD) + cached_key_rows.shape[2:]
    copies = jnp.broadcast_to(rows_here[None], (width, batch, features))
    pieces = lax.all_to_all(copies, "tp", 0, 0)
    gathered = pieces.transpose(1, 0, 2).reshape(batch, width * features)
    wide = gathered.astype(jnp.float32)
    inverse = lax.rsqrt(jnp.mean(wide * wide, axis=-1, keepdims=True) + EPS)
    normed = (wide * inverse * attention_norm_scale).astype(jnp.bfloat16)
    shrunk = jnp.dot(normed, adapter_down_weight[0, 0], preferred_element_type=jnp.float32)
    picked = jnp.dot(
        mine.astype(jnp.bfloat16), shrunk.astype(jnp.bfloat16), preferred_element_type=jnp.float32
    ).astype(jnp.bfloat16)
    update = jnp.dot(picked, adapter_up_weight[0, 0], preferred_element_type=jnp.float32)
    columns = update.shape[1] // width
    update = (update * ADAPTER_SCALE).astype(jnp.bfloat16).reshape(MOST, width, columns)
    update = jnp.pad(update.transpose(1, 0, 2), ((0, 0), (0, 0), (0, 3 * HD - columns)))
    update = jnp.pad(update.reshape(width, 3 * MOST, HD), ((0, 0), (0, 8 - 3 * MOST), (0, 0)))
    received = lax.all_to_all(update, "tp", 0, 0)
    base = jnp.dot(normed, joined_projection_weight[0], preferred_element_type=jnp.float32)
    base = jnp.pad(base, ((0, 0), (0, 3 * HD - base.shape[1])))
    (slots,) = call(
        pack_kernel,
        4,
        (jax.ShapeDtypeStruct((TP, SLOT, HD), jnp.bfloat16),),
        [],
        base,
        spread,
        received,
        *[Far(part) for part in given],
    )
    joined = lax.all_to_all(slots, "tp", 0, 0)

    sent, moved_rows = call(
        attention_kernel,
        12,
        (pltpu.HBM((TP, PART, HD), jnp.bfloat16), pltpu.HBM((batch, features), jnp.bfloat16)),
        [
            pltpu.VMEM((TP, LINES, HD), jnp.float32),
            pltpu.VMEM((2 * KVH, LINES, HD), jnp.float32),
            pltpu.VMEM((TP, LINES, HD), jnp.float32),
            pltpu.VMEM((2, 8, HD), jnp.float32),
            pltpu.VMEM((8, HD), jnp.float32),
            pltpu.VMEM((QUADS, 2 * QUAD * SPAN, HD), jnp.float32),
            pltpu.VMEM(near_cache, jnp.bfloat16),
            pltpu.VMEM(near_cache, jnp.bfloat16),
            pltpu.VMEM((TP, PART, HD), jnp.bfloat16),
            pltpu.SemaphoreType.DMA((2, QUADS)),
            pltpu.SemaphoreType.DMA((2, 2 * QUADS)),
            pltpu.SemaphoreType.DMA((2,)),
            pltpu.SemaphoreType.DMA,
        ],
        joined,
        limits,
        Far(cached_key_rows[0]),
        Far(cached_value_rows[0]),
        *[Far(part) for part in given],
        moved_rows,
    )
    arrived = lax.all_to_all(sent, "tp", 0, 0)
    (context,) = call(combine_kernel, 4, (jax.ShapeDtypeStruct((ROWS * HEADS_HERE, HD), jnp.float32),), [], arrived)
    context = context.reshape(batch, HEADS_HERE * HD).astype(jnp.bfloat16)
    moved_context = passed_along(context, "section", 1)
    return (moved_rows[None], moved_context[None])


def solution(mesh):
    return jax.shard_map(
        on_device,
        mesh=mesh,
        in_specs=(
            P("section", None, "tp"),
            P(),
            P("section", None, "tp"),
            P("section", "tp", None, None),
            P("section", "tp", None, None),
            P("section", None, "tp", None),
            P("section", None, "tp", None),
            P("section", None, None),
            P("section", None),
        ),
        out_specs=(P("section", None, "tp"), P("section", None, "tp")),
        check_vma=False,
    )
```

time: 96.1 us -> 91.2 us (0.949)
  waiting for transfers between devices: 37.6 us -> 28.6 us
  starting transfers between devices: 20.9 us -> 26.9 us
  blocking collectives: 19.3 us -> 15.7 us
  local copies, waits for them, and re-layouts: 4.01 us -> 6.46 us
  other arithmetic: 2.72 us -> 0.86 us
  matrix products: 4.79 us -> 6.03 us
    ppermute x0 -> x4, starting transfers between devices: none -> 4.75 us  [on_device(): given.append(lax.ppermute(part, 'tp', pairs))]
    ppermute x2, waiting for transfers between devices: 8.63 us -> 4.32 us  [passed_along(): lax.ppermute(array, axis, [(i, (i + by) % devices) for i in range(devices)])]
    all_to_all x1, waiting for transfers between devices: 11.8 us -> 7.55 us  [on_device(): pieces = lax.all_to_all(copies, 'tp', 0, 0)]
    all_to_all x1, blocking collectives: 19.3 us -> 15.7 us  [on_device(): arrived = lax.all_to_all(sent, 'tp', 0, 0)]
    dynamic_slice x0 -> x2, local copies, waits for them, and re-layouts: none -> 3.06 us  [on_device(): lax.dynamic_slice_in_dim(cached, SHARE * (1 - side) + GIVEN * i, GIVEN, 0)]
    dot_general x1, matrix products: 0.51 us -> 1.74 us  [on_device(): jnp.dot(mine.astype(jnp.bfloat16), shrunk.astype(jnp.bfloat16), preferred...]
  transfers between devices with their start and end apart: 5 -> 9, of which waited for: 5 -> 4; matrix products, arithmetic and copies ran while one was open for 7% -> 14% of each run, Pallas kernels for 0% -> 1%
where the time goes in v3:
time: 91.2 us; the launch traced here: 90.6 us
  waiting for transfers between devices  28.6 us (31%)
  starting transfers between devices  26.9 us (29%)
  blocking collectives  15.7 us (17%)
  local copies, waits for them, and re-layouts  6.46 us (7%)
  matrix products  6.03 us (7%)
  Pallas kernels  5.05 us (6%)
  between operations  0.94 us (1%)
    all_to_all x1, blocking collectives, on_device(): arrived = lax.all_to_all(sent, 'tp', 0, 0)  15.7 us
    all_to_all x1, waiting for transfers between devices, on_device(): joined = lax.all_to_all(slots, 'tp', 0, 0)  11.7 us
    all_to_all x1, starting transfers between devices, on_device(): pieces = lax.all_to_all(copies, 'tp', 0, 0)  11.4 us
    all_to_all x1, waiting for transfers between devices, on_device(): pieces = lax.all_to_all(copies, 'tp', 0, 0)  7.55 us
    all_to_all x1, starting transfers between devices, on_device(): joined = lax.all_to_all(slots, 'tp', 0, 0)  5.65 us
    all_to_all x1, starting transfers between devices, on_device(): received = lax.all_to_all(update, 'tp', 0, 0)  5.1 us
    pallas_call x3, Pallas kernels, call(): pl.pallas_call(kernel, out_shape=out_shape, in_specs=[hbm if f else vmem...  5.05 us
    all_to_all x1, waiting for transfers between devices, on_device(): received = lax.all_to_all(update, 'tp', 0, 0)  5.02 us
  transfers between devices with their start and end apart: 9, of which 4 were waited for; matrix products, arithmetic and copies ran while one was open for 14% of the time, Pallas kernels for 1%

profile of v3, /device:TPU:32, one launch (start us, length us, event | category | flops | bytes accessed | tf_op | source)
XLA Modules:
  0.0 90.6 jit_solution(13264302372147378071)
XLA Ops:
  0.6 0.0 copy-start
  0.6 0.0 copy-start.1
  0.7 0.0 collective-permute-start.4
  0.7 1.6 %broadcast_in_dim.19 = bf16[32,24,256]{2,1,0:T(8,128)(2,1)} broadcast(bf16[24,256]{1,0:T(8,128)(2,1)} %bitcast.54), dimensions={1,2} | broadcast | bytes 405504 | tf_op jit(solution)/shard_map/broadcast_in_dim | solution.py:314
  2.3 11.4 %all-to-all-start = ((bf16[32,24,256]{2,1,0:T(8,128)(2,1)}), bf16[32,24,256]{2,1,0:T(8,128)(2,1)S(1)}, u32[]{:S(2)}, u32[]{:S(2)}) async-start(bf16[32,24,256]{2,1,0:T(8,128)(2,1)} %broadcast_in_dim.19), calls=%async_computation | async-start | bytes 786432 | tf_op jit(solution)/shard_map/all_to_all | solution.py:315
  13.7 0.0 copy-start.5
  13.7 0.0 copy-start.4
  13.7 0.0 copy-start.6
  13.8 2.1 %dynamic-slice_bitcast_fusion.2 = (bf16[6,32,1024]{2,1,0:T(8,128)(2,1)}, bf16[6,32,1024]{2,1,0:T(8,128)(2,1)}) fusion(bf16[1,24,32,1024]{3,2,1,0:T(8,128)(2,1)} %param.14, s32[]{:T(128)S(6)} %select_n.45, s32[]{:T(128)S(6)} %select_n.44), kind=kLoop, calls=%fused_computation.17 | loop fusion | bytes 1572872 | tf_op jit(solution)/shard_map/dynamic_slice | solution.py:302
  15.9 1.5 %collective-permute-start = (bf16[6,32,1024]{2,1,0:T(8,128)(2,1)}, bf16[6,32,1024]{2,1,0:T(8,128)(2,1)}, u32[]{:S(2)}, u32[]{:S(2)}) collective-permute-start(bf16[6,32,1024]{2,1,0:T(8,128)(2,1)} %get-tuple-element.11), channel_id=1, source_target_pairs={{0,8},{1,9},{2,10},{3,11},{4,12},{5,13},{6,14},{7,15},{8,0},{9,1},... | collective-permute-start | bytes 1179656 | tf_op jit(solution)/shard_map/ppermute | solution.py:303
  17.3 2.1 %collective-permute-start.1 = (bf16[6,32,1024]{2,1,0:T(8,128)(2,1)}, bf16[6,32,1024]{2,1,0:T(8,128)(2,1)}, u32[]{:S(2)}, u32[]{:S(2)}) collective-permute-start(bf16[6,32,1024]{2,1,0:T(8,128)(2,1)} %get-tuple-element.10), channel_id=1, source_target_pairs={{0,24},{1,25},{2,26},{3,27},{4,28},{5,29},{6,30},{7,31},{8,16},{9,... | collective-permute-start | bytes 1179656 | tf_op jit(solution)/shard_map/ppermute | solution.py:303
  19.4 0.0 copy-done.1
  19.4 1.0 %dynamic-slice_bitcast_fusion = (bf16[6,32,1024]{2,1,0:T(8,128)(2,1)}, bf16[6,32,1024]{2,1,0:T(8,128)(2,1)}) fusion(bf16[1,24,32,1024]{3,2,1,0:T(8,128)(2,1)S(1)} %copy-done.1, s32[]{:T(128)S(6)} %select_n.45, s32[]{:T(128)S(6)} %select_n.44), kind=kLoop, calls=%fused_computation.15 | loop fusion | bytes 1572872 | tf_op jit(solution)/shard_map/dynamic_slice | solution.py:302
  20.4 0.6 collective-permute-start.2
  21.0 0.6 collective-permute-start.3
  21.6 0.0 copy-done.5
  21.6 0.1 slice_bitcast_fusion
  21.7 0.1 slice_bitcast_fusion.1
  21.8 0.2 convert_reduce_fusion
  22.0 0.1 fusion.12.spread_ref
  22.1 7.5 %all-to-all-done = bf16[32,24,256]{2,1,0:T(8,128)(2,1)S(1)} async-done(((bf16[32,24,256]{2,1,0:T(8,128)(2,1)}), bf16[32,24,256]{2,1,0:T(8,128)(2,1)S(1)}, u32[]{:S(2)}, u32[]{:S(2)}) %all-to-all-start) | async-done | bytes 393248 | tf_op jit(solution)/shard_map/all_to_all | solution.py:315
  29.6 0.2 fusion.8
  29.8 0.2 fusion.11
  30.1 1.7 %fusion.5 = bf16[2,64]{1,0:T(2,128)(2,1)S(1)} fusion(bf16[24,8192]{1,0:T(8,128)(2,1)S(1)} %bitcast.50, bf16[1,1,8192,64]{2,3,1,0:T(8,128)(2,1)} %param.12, pred[24]{0:T(512)(128)(4,1)S(1)} %broadcast_compare_fusion, s32[24]{0:T(128)S(1)} %convert_reduce_fusion), kind=kOutput, calls=%fused_computation.7 | convolution fusion | flops 25173728 | bytes 1442168 | tf_op jit(solution)/shard_map/dot_general | solution.py:321
  31.8 0.3 fusion
  32.1 0.1 reshape.94
  32.3 0.6 pad.14
  33.0 5.1 %all-to-all-start.1 = ((bf16[32,8,128]{2,1,0:T(8,128)(2,1)}), bf16[32,8,128]{2,1,0:T(8,128)(2,1)S(1)}, u32[]{:S(2)}, u32[]{:S(2)}) async-start(bf16[32,8,128]{2,1,0:T(8,128)(2,1)} %pad.14), calls=%async_computation.1 | async-start | bytes 131072 | tf_op jit(solution)/shard_map/all_to_all | solution.py:329
  38.1 4.0 %fusion.1 = f32[24,320]{1,0:T(8,128)S(1)} fusion(bf16[24,8192]{1,0:T(8,128)(2,1)S(1)} %bitcast.51, bf16[1,8192,320]{1,2,0:T(8,128)(2,1)} %param.11), kind=kOutput, calls=%fused_computation.2 | convolution fusion | flops 125829120 | bytes 5666816 | tf_op jit(solution)/shard_map/dot_general | solution.py:330
  42.1 0.0 collective-permute-done.rest_0_.keys_a
  42.1 0.0 collective-permute-done.1.rest_1_.keys_b
  42.1 0.0 collective-permute-done.2.rest_2_.values_a
  42.1 0.0 collective-permute-done.3.rest_3_.values_b
  42.2 0.0 copy-start.3
  42.2 5.0 %all-to-all-done.1.received_ref = bf16[32,8,128]{2,1,0:T(8,128)(2,1)S(1)} async-done(((bf16[32,8,128]{2,1,0:T(8,128)(2,1)}), bf16[32,8,128]{2,1,0:T(8,128)(2,1)S(1)}, u32[]{:S(2)}, u32[]{:S(2)}) %all-to-all-start.1) | async-done | bytes 65568 | tf_op jit(solution)/shard_map/all_to_all | solution.py:329
  47.2 1.0 %shard_map.104 = bf16[32,32,128]{2,1,0:T(8,128)(2,1)} custom-call(f32[24,384]{1,0:T(8,128)S(1)} %pad.12.base_ref, bf16[3,24,256]{2,1,0:T(8,128)(2,1)S(1)} %fusion.12.spread_ref, bf16[32,8,128]{2,1,0:T(8,128)(2,1)S(1)} %all-to-all-done.1.received_ref, bf16[6,32,1024]{2,1,0:T(8,128)(2,1)} %collective-permute-done.rest_0_.keys_a, ...), custom_call_target="tpu_custom_call" | custom-call | tf_op jit(solution)/shard_map/pallas_call | solution.py:43
  48.1 5.6 %all-to-all-start.2 = ((bf16[32,32,128]{2,1,0:T(8,128)(2,1)}), bf16[32,32,128]{2,1,0:T(8,128)(2,1)S(1)}, u32[]{:S(2)}, u32[]{:S(2)}) async-start(bf16[32,32,128]{2,1,0:T(8,128)(2,1)} %shard_map.104), calls=%async_computation.2 | async-start | bytes 524288 | tf_op jit(solution)/shard_map/all_to_all | solution.py:342
  53.8 0.1 broadcast_subtract_fusion
  53.9 0.1 pad_add_fusion
  54.0 0.0 collective-permute-done.4.moved_ref
  54.0 11.7 %all-to-all-done.2.slots_ref = bf16[32,32,128]{2,1,0:T(8,128)(2,1)S(1)} async-done(((bf16[32,32,128]{2,1,0:T(8,128)(2,1)}), bf16[32,32,128]{2,1,0:T(8,128)(2,1)S(1)}, u32[]{:S(2)}, u32[]{:S(2)}) %all-to-all-start.2) | async-done | bytes 262176 | tf_op jit(solution)/shard_map/all_to_all | solution.py:342
  65.7 0.1 broadcast_in_dim.40.limit_ref
  65.8 3.6 %shard_map.105 = (bf16[32,32,128]{2,1,0:T(8,128)(2,1)}, bf16[24,256]{1,0:T(8,128)(2,1)}) custom-call(bf16[32,32,128]{2,1,0:T(8,128)(2,1)S(1)} %all-to-all-done.2.slots_ref, s32[24,128]{1,0:T(8,128)S(1)} %broadcast_in_dim.40.limit_ref, bf16[24,32,1024]{2,1,0:T(8,128)(2,1)} %bitcast.48, bf16[24,32,1024]{2,1,0:T(8,128)(2,1)} %bitcast.49, ...), custom_call_target="tpu_custom_call" | custom-call | tf_op jit(solution)/shard_map/pallas_call | solution.py:43
  69.4 15.7 %all_to_all.20.arrived_ref = bf16[32,32,128]{2,1,0:T(8,128)(2,1)S(1)} all-to-all(bf16[32,32,128]{2,1,0:T(8,128)(2,1)} %get-tuple-element.5), channel_id=1, replica_groups=mesh['section'=8,'tp'=32] {'tp'}, dimensions={0} | all-to-all | bytes 524288 | tf_op jit(solution)/shard_map/all_to_all | solution.py:370
  85.1 0.5 shard_map.106
  85.7 0.0 collective-permute-start.5
  85.7 4.3 %collective-permute-done.5 = bf16[24,256]{1,0:T(8,128)(2,1)S(1)} collective-permute-done((bf16[24,256]{1,0:T(8,128)(2,1)S(1)}, bf16[24,256]{1,0:T(8,128)(2,1)S(1)}, u32[]{:S(2)}, u32[]{:S(2)}) %collective-permute-start.5) | collective-permute-done | bytes 12320 | tf_op jit(solution)/shard_map/ppermute | solution.py:36
  90.0 0.6 copy.21
  (19 shorter events, 0.2 us)
Async XLA Ops:
  0.6 31.2 %copy-start = (bf16[1,1,64,10240]{3,2,1,0:T(8,128)(2,1)S(1)}, bf16[1,1,64,10240]{3,2,1,0:T(8,128)(2,1)}, u32[]{:S(2)}) copy-start(bf16[1,1,64,10240]{3,2,1,0:T(8,128)(2,1)} %param.13) | copy-start | bytes 3932164
  0.6 18.7 %copy-start.1 = (bf16[1,24,32,1024]{3,2,1,0:T(8,128)(2,1)S(1)}, bf16[1,24,32,1024]{3,2,1,0:T(8,128)(2,1)}, u32[]{:S(2)}) copy-start(bf16[1,24,32,1024]{3,2,1,0:T(8,128)(2,1)} %param.15) | copy-start | bytes 4718596
  0.7 53.3 %collective-permute-start.4 = (bf16[24,256]{1,0:T(8,128)(2,1)}, bf16[24,256]{1,0:T(8,128)(2,1)S(1)}, u32[]{:S(2)}, u32[]{:S(2)}) collective-permute-start(bf16[24,256]{1,0:T(8,128)(2,1)} %bitcast.53), channel_id=1, source_target_pairs={{0,32},{32,64},{64,96},{96,128},{128,160},{160,192},{192,224},{224... | collective-permute-start | bytes 36872 | tf_op jit(solution)/shard_map/ppermute | solution.py:36
  2.3 27.3 %all-to-all-start = ((bf16[32,24,256]{2,1,0:T(8,128)(2,1)}), bf16[32,24,256]{2,1,0:T(8,128)(2,1)S(1)}, u32[]{:S(2)}, u32[]{:S(2)}) async-start(bf16[32,24,256]{2,1,0:T(8,128)(2,1)} %broadcast_in_dim.19), calls=%async_computation | async-start | bytes 786432 | tf_op jit(solution)/shard_map/all_to_all | solution.py:315
  13.7 7.9 %copy-start.5 = (s32[1,24]{1,0:T(1,128)S(1)}, s32[1,24]{1,0:T(1,128)}, u32[]{:S(2)}) copy-start(s32[1,24]{1,0:T(1,128)} %param.17) | copy-start | bytes 292
  13.7 8.0 %copy-start.4 = (f32[8192]{0:T(1024)S(1)}, f32[8192]{0:T(1024)}, u32[]{:S(2)}) copy-start(f32[8192]{0:T(1024)} %param.10) | copy-start | bytes 98308
  13.7 8.0 %copy-start.6 = (s32[1,24,1]{1,2,0:T(1,128)S(1)}, s32[1,24,1]{1,2,0:T(1,128)}, u32[]{:S(2)}) copy-start(s32[1,24,1]{1,2,0:T(1,128)} %param.16) | copy-start | bytes 292
  15.9 26.3 %collective-permute-start = (bf16[6,32,1024]{2,1,0:T(8,128)(2,1)}, bf16[6,32,1024]{2,1,0:T(8,128)(2,1)}, u32[]{:S(2)}, u32[]{:S(2)}) collective-permute-start(bf16[6,32,1024]{2,1,0:T(8,128)(2,1)} %get-tuple-element.11), channel_id=1, source_target_pairs={{0,8},{1,9},{2,10},{3,11},{4,12},{5,13},{6,14},{7,15},{8,0},{9,1},... | collective-permute-start | bytes 1179656 | tf_op jit(solution)/shard_map/ppermute | solution.py:303
  17.3 24.8 %collective-permute-start.1 = (bf16[6,32,1024]{2,1,0:T(8,128)(2,1)}, bf16[6,32,1024]{2,1,0:T(8,128)(2,1)}, u32[]{:S(2)}, u32[]{:S(2)}) collective-permute-start(bf16[6,32,1024]{2,1,0:T(8,128)(2,1)} %get-tuple-element.10), channel_id=1, source_target_pairs={{0,24},{1,25},{2,26},{3,27},{4,28},{5,29},{6,30},{7,31},{8,16},{9,... | collective-permute-start | bytes 1179656 | tf_op jit(solution)/shard_map/ppermute | solution.py:303
  20.4 21.8 %collective-permute-start.2 = (bf16[6,32,1024]{2,1,0:T(8,128)(2,1)}, bf16[6,32,1024]{2,1,0:T(8,128)(2,1)S(1)}, u32[]{:S(2)}, u32[]{:S(2)}) collective-permute-start(bf16[6,32,1024]{2,1,0:T(8,128)(2,1)} %get-tuple-element.9), channel_id=1, source_target_pairs={{0,8},{1,9},{2,10},{3,11},{4,12},{5,13},{6,14},{7,15},{8,0},{9,1},... | collective-permute-start | bytes 1179656 | tf_op jit(solution)/shard_map/ppermute | solution.py:303
  21.0 21.2 %collective-permute-start.3 = (bf16[6,32,1024]{2,1,0:T(8,128)(2,1)}, bf16[6,32,1024]{2,1,0:T(8,128)(2,1)S(1)}, u32[]{:S(2)}, u32[]{:S(2)}) collective-permute-start(bf16[6,32,1024]{2,1,0:T(8,128)(2,1)} %get-tuple-element.8), channel_id=1, source_target_pairs={{0,24},{1,25},{2,26},{3,27},{4,28},{5,29},{6,30},{7,31},{8,16},{9,... | collective-permute-start | bytes 1179656 | tf_op jit(solution)/shard_map/ppermute | solution.py:303
  33.0 14.2 %all-to-all-start.1 = ((bf16[32,8,128]{2,1,0:T(8,128)(2,1)}), bf16[32,8,128]{2,1,0:T(8,128)(2,1)S(1)}, u32[]{:S(2)}, u32[]{:S(2)}) async-start(bf16[32,8,128]{2,1,0:T(8,128)(2,1)} %pad.14), calls=%async_computation.1 | async-start | bytes 131072 | tf_op jit(solution)/shard_map/all_to_all | solution.py:329
  42.1 5.0 %copy-start.2 = (bf16[6,32,1024]{2,1,0:T(8,128)(2,1)}, bf16[6,32,1024]{2,1,0:T(8,128)(2,1)S(1)}, u32[]{:S(2)}) copy-start(bf16[6,32,1024]{2,1,0:T(8,128)(2,1)S(1)} %collective-permute-done.2.rest_2_.values_a) | copy-start | bytes 1179652
  42.2 5.0 %copy-start.3 = (bf16[6,32,1024]{2,1,0:T(8,128)(2,1)}, bf16[6,32,1024]{2,1,0:T(8,128)(2,1)S(1)}, u32[]{:S(2)}) copy-start(bf16[6,32,1024]{2,1,0:T(8,128)(2,1)S(1)} %collective-permute-done.3.rest_3_.values_b) | copy-start | bytes 1179652
  48.1 17.6 %all-to-all-start.2 = ((bf16[32,32,128]{2,1,0:T(8,128)(2,1)}), bf16[32,32,128]{2,1,0:T(8,128)(2,1)S(1)}, u32[]{:S(2)}, u32[]{:S(2)}) async-start(bf16[32,32,128]{2,1,0:T(8,128)(2,1)} %shard_map.104), calls=%async_computation.2 | async-start | bytes 524288 | tf_op jit(solution)/shard_map/all_to_all | solution.py:342
  85.7 4.3 %collective-permute-start.5 = (bf16[24,256]{1,0:T(8,128)(2,1)S(1)}, bf16[24,256]{1,0:T(8,128)(2,1)S(1)}, u32[]{:S(2)}, u32[]{:S(2)}) collective-permute-start(bf16[24,256]{1,0:T(8,128)(2,1)S(1)} %convert_element_type.55), channel_id=1, source_target_pairs={{0,32},{32,64},{64,96},{96,128},{128,160},{160,192},{192,224},{224... | collective-permute-start | bytes 36872 | tf_op jit(solution)/shard_map/ppermute | solution.py:36

commit v4 on v3

--- a/solution.py
+++ b/solution.py
@@ -38,12 +38,17 @@
 
 def call(kernel, mebibytes, out_shape, scratch, *arguments):
     vmem, hbm = pl.BlockSpec(memory_space=pltpu.VMEM), pl.BlockSpec(memory_space=pltpu.HBM)
-    far = [isinstance(a, Far) for a in arguments]
-    values = [pltpu.with_memory_space_constraint(a.array, pltpu.HBM) if f else a for a, f in zip(arguments, far)]
+    specs, values = [], []
+    for a in arguments:
+        far = isinstance(a, Far)
+        specs.append(pl.BlockSpec(memory_space=a.space) if far else vmem)
+        values.append(a.array if far else a)
+        if far and a.space == pltpu.HBM:
+            values[-1] = pltpu.with_memory_space_constraint(a.array, pltpu.HBM)
     return pl.pallas_call(
         kernel,
         out_shape=out_shape,
-        in_specs=[hbm if f else vmem for f in far],
+        in_specs=specs,
         out_specs=tuple(hbm if getattr(o, "memory_space", None) == pltpu.HBM else vmem for o in out_shape),
         scratch_shapes=scratch,
         compiler_params=pltpu.CompilerParams(vmem_limit_bytes=mebibytes * 1024 * 1024),
@@ -51,8 +56,8 @@
 
 
 class Far:
-    def __init__(self, array):
-        self.array = array
+    def __init__(self, array, space=pltpu.HBM):
+        self.array, self.space = array, space
 
 
 def low_lanes(shape):
@@ -93,34 +98,27 @@
 
 
 def attention_kernel(
-    slots_ref, limit_ref, keys_far, values_far, keys_a, keys_b, values_a, values_b, moved_ref, sent_ref, kept_ref,
-    query, fresh, result, levels, added, biases, keys_ref, values_ref, sent, load_sem, given_sem, sent_sem, kept_sem,
+    slots_ref, used_ref, keys_own, values_far, keys_a, keys_b, values_a, values_b, moved_ref, sent_ref, kept_ref,
+    query, fresh, result, levels, added, biases, values_own, given_va, given_vb, load_sem, kept_sem,
 ):
     device = lax.axis_index("tp")
     side = device // NEAR % 2
-    caches = ((keys_far, keys_a, keys_b, keys_ref), (values_far, values_a, values_b, values_ref))
-
-    def own_load(i, q):
-        start = SHARE * side + QUAD * lax.rem(q + side, QUADS)
-        far, near = caches[i][0], caches[i][3]
-        return pltpu.make_async_copy(far.at[pl.ds(start, QUAD)], near.at[q, 0], load_sem.at[i, q])
-
-    def given_load(i, p, on_side):
-        row = (2 * p + QUAD * on_side) % SHARE
-        far, near = caches[i][1 + row // GIVEN], caches[i][3]
-        return pltpu.make_async_copy(
-            far.at[pl.ds(row % GIVEN, 2)], near.at[p // 2, 1, pl.ds(2 * (p % 2), 2)], given_sem.at[i, p]
-        )
-
-    for i in range(2):
-        for q in range(QUADS):
-            own_load(i, q).start()
-        for on_side in range(2):
-
-            @pl.when(side == on_side)
-            def _():
-                for p in range(2 * QUADS):
-                    given_load(i, p, on_side).start()
+    first_giver = device + NEAR - 2 * NEAR * side
+    second_giver = (TP // NEAR - 1 - device // NEAR) * NEAR + device % NEAR
+    loads = [
+        pltpu.make_async_copy(values_far.at[pl.ds(SHARE * side, SHARE)], values_own, load_sem.at[0]),
+        pltpu.make_async_copy(values_a, given_va, load_sem.at[1]),
+        pltpu.make_async_copy(values_b, given_vb, load_sem.at[2]),
+    ]
+    for load in loads:
+        load.start()
+
+    def lined_up(own, given_a, given_b, q, lanes):
+        parts = [own[QUAD * q : QUAD * (q + 1), :, lanes]]
+        for row in range(QUAD * q, QUAD * (q + 1), 2):
+            given, at = (given_a, row) if row < GIVEN else (given_b, row - GIVEN)
+            parts.append(given[at : at + 2, :, lanes])
+        return jnp.concatenate([part.reshape(-1, part.shape[-1]) for part in parts], axis=0)
 
     keep = pltpu.make_async_copy(moved_ref, kept_ref, kept_sem)
     keep.start()
@@ -130,16 +128,16 @@
     position = lax.broadcasted_iota(jnp.int32, (SPAN, HD), 0)
     for block in range(2):
         for row in range(SHARE):
-            at = block * SHARE + row
-            seen = (position < limit_ref[at : at + 1, :]) & (row_lane == row % QUAD)
+            start = (device, first_giver if row < GIVEN else second_giver)[block] * SPAN
+            seen = (position < used_ref[SHARE * side + row] - start) & (row_lane == row % QUAD)
             to = SPAN * (QUAD * block + row % QUAD)
             biases[row // QUAD, to : to + SPAN, :] = jnp.where(seen, 0.0, NEGATIVE)
     low = low_lanes((8, HD))
 
     def put(head, main, left):
-        def store(ref, at, side):
-            ref[at, pl.ds(side, 8, stride=2), :] = main
-            ref[at, pl.ds(16 + side, 4, stride=2), :] = left[0:4]
+        def store(ref, at, which):
+            ref[at, pl.ds(8 * side + which, 8, stride=2), :] = main
+            ref[at, pl.ds(16 - 16 * side + which, 4, stride=2), :] = left[0:4]
 
         if head < H:
             store(query, head // 2, head % 2)
@@ -158,7 +156,7 @@
 
     eighth = lax.broadcasted_iota(jnp.int32, (8, HD), 1) // 8
     eye = lax.broadcasted_iota(jnp.int32, (8, HD), 0) == lax.broadcasted_iota(jnp.int32, (8, HD), 1)
-    own_devices = (device, device + NEAR - 2 * NEAR * side)
+    own_devices = (device, first_giver)
     own_lines = jnp.full((8, HD), NEGATIVE, jnp.float32)
     for at in own_devices:
         own = query[at] * fresh[at // (TP // KVH)]
@@ -169,12 +167,7 @@
         lines = jnp.concatenate(lines + [jnp.zeros((8 - QUADS, HD), jnp.float32)], axis=0)
         own_lines = jnp.where(eighth == at % 16, pltpu.roll(lines, 8 * (at % 16), 1), own_lines)
 
-    rows = 2 * QUAD * SPAN
     lane = lax.broadcasted_iota(jnp.int32, (HD, HD), 1)
-    for q in range(QUADS):
-        own_load(0, q).wait()
-    for p in range(2 * QUADS):
-        given_load(0, p, 0).wait()
     kept = {}
     for gg in range(2):
         own_here = jnp.where(device // 16 == gg, own_lines, NEGATIVE)
@@ -183,7 +176,7 @@
             turned = jnp.transpose(left)
             parts = [jnp.where(lane // 32 == i, turned, 0.0).astype(jnp.bfloat16) for i in range(4)]
             right = jnp.concatenate(parts, axis=0)
-            keys = keys_ref[q, :, :, :, 512 * gg : 512 * (gg + 1)].reshape(rows, 512)
+            keys = lined_up(keys_own, keys_a, keys_b, q, slice(512 * gg, 512 * (gg + 1)))
             scores = jnp.dot(keys, right, preferred_element_type=jnp.float32) * FACTOR + biases[q]
             own = own_here[q : q + 1, :]
             top = jnp.maximum(jnp.maximum(jnp.max(scores, axis=0, keepdims=True), own), FLOOR)
@@ -203,11 +196,8 @@
         value = fresh[KVH + at // (TP // KVH)]
         terms = [columns[0:8, q : q + 1] * value[8 * q : 8 * q + 8] for q in range(QUADS)]
         own_terms.append(jnp.concatenate(terms, axis=0))
-    for q in range(QUADS):
-        own_load(1, q).wait()
-    for p in range(2 * QUADS):
-        given_load(1, p, 0).wait()
-    stores = []
+    for load in loads:
+        load.wait()
     for gg in range(2):
         level = levels[gg]
         high = level.astype(jnp.bfloat16).astype(jnp.float32)
@@ -217,7 +207,7 @@
         for q in range(QUADS):
             for i in range(4):
                 g = 4 * gg + i
-                part = values_ref[q, :, :, :, g * HD : (g + 1) * HD].reshape(rows, HD)
+                part = lined_up(values_own, given_va, given_vb, q, slice(g * HD, (g + 1) * HD))
                 mixed = jnp.dot(kept[gg, q][32 * i : 32 * i + 32], part, preferred_element_type=jnp.float32)
                 for j in range(4):
                     result[4 * g + j, 8 * q : 8 * q + 8, :] = mixed[8 * j : 8 * j + 8]
@@ -227,12 +217,7 @@
             whole = result[t]
             for at, terms in zip(own_devices, own_terms):
                 whole = whole + jnp.where(at == t, terms, 0.0)
-            sent[t] = jnp.concatenate([whole, lines], axis=0).astype(jnp.bfloat16)
-        half = pl.ds(16 * gg, 16)
-        stores.append(pltpu.make_async_copy(sent.at[half], sent_ref.at[half], sent_sem.at[gg]))
-        stores[-1].start()
-    for store in stores:
-        store.wait()
+            sent_ref[t] = jnp.concatenate([whole, lines], axis=0).astype(jnp.bfloat16)
     keep.wait()
 
 
@@ -262,7 +247,7 @@
             for q in range(QUADS):
                 at = 8 * i + q
                 totals[q] = totals[q] + columns[0:8, at : at + 1] * rows[8 * q : 8 * q + 8]
-        pieces += totals if side == 0 else [totals[2], totals[0], totals[1]]
+        pieces += totals
     context_ref[...] = jnp.concatenate(pieces, axis=0)
 
 
@@ -302,15 +287,7 @@
             part = lax.dynamic_slice_in_dim(cached, SHARE * (1 - side) + GIVEN * i, GIVEN, 0)
             given.append(lax.ppermute(part, "tp", pairs))
     span = cached_key_rows.shape[2]
-    used = lengths[0]
-    turned = jnp.concatenate([used[SHARE + QUAD :], used[SHARE : SHARE + QUAD]])
-    used = jnp.where(side == 0, used[:SHARE], turned)
-    row = (jnp.arange(SHARE) + QUAD * side) % SHARE
-    y, z = device // NEAR, device % NEAR
-    giver = jnp.where(row < GIVEN, y ^ 1, wide - 1 - y) * NEAR + z
-    limits = jnp.concatenate([used - span * device, used - span * giver])
-    limits = jnp.broadcast_to(limits[:, None], (2 * SHARE, HD))
-    near_cache = (QUADS, 2, QUAD) + cached_key_rows.shape[2:]
+    own_keys = lax.dynamic_slice_in_dim(cached_key_rows[0], SHARE * side, SHARE, 0)
     copies = jnp.broadcast_to(rows_here[None], (width, batch, features))
     pieces = lax.all_to_all(copies, "tp", 0, 0)
     gathered = pieces.transpose(1, 0, 2).reshape(batch, width * features)
@@ -337,14 +314,15 @@
         base,
         spread,
         received,
-        *[Far(part) for part in given],
+        *[Far(part, pl.ANY) for part in (*given[:2], own_keys, moved_rows)],
+        *[Far(part) for part in given[2:]],
     )
     joined = lax.all_to_all(slots, "tp", 0, 0)
 
     sent, moved_rows = call(
         attention_kernel,
         12,
-        (pltpu.HBM((TP, PART, HD), jnp.bfloat16), pltpu.HBM((batch, features), jnp.bfloat16)),
+        (jax.ShapeDtypeStruct((TP, PART, HD), jnp.bfloat16), pltpu.HBM((batch, features), jnp.bfloat16)),
         [
             pltpu.VMEM((TP, LINES, HD), jnp.float32),
             pltpu.VMEM((2 * KVH, LINES, HD), jnp.float32),
@@ -352,19 +330,18 @@
             pltpu.VMEM((2, 8, HD), jnp.float32),
             pltpu.VMEM((8, HD), jnp.float32),
             pltpu.VMEM((QUADS, 2 * QUAD * SPAN, HD), jnp.float32),
-            pltpu.VMEM(near_cache, jnp.bfloat16),
-            pltpu.VMEM(near_cache, jnp.bfloat16),
-            pltpu.VMEM((TP, PART, HD), jnp.bfloat16),
-            pltpu.SemaphoreType.DMA((2, QUADS)),
-            pltpu.SemaphoreType.DMA((2, 2 * QUADS)),
-            pltpu.SemaphoreType.DMA((2,)),
+            pltpu.VMEM((SHARE, span, KVH * HD), jnp.bfloat16),
+            pltpu.VMEM((GIVEN, span, KVH * HD), jnp.bfloat16),
+            pltpu.VMEM((GIVEN, span, KVH * HD), jnp.bfloat16),
+            pltpu.SemaphoreType.DMA((3,)),
             pltpu.SemaphoreType.DMA,
         ],
         joined,
-        limits,
-        Far(cached_key_rows[0]),
+        Far(lengths[0], pltpu.SMEM),
+        own_keys,
         Far(cached_value_rows[0]),
-        *[Far(part) for part in given],
+        *given[:2],
+        *[Far(part) for part in given[2:]],
         moved_rows,
     )
     arrived = lax.all_to_all(sent, "tp", 0, 0)

time: 91.2 us -> 88.3 us (0.968)
  blocking collectives: 15.7 us -> 32 us
  waiting for transfers between devices: 28.6 us -> 15.7 us
  starting transfers between devices: 26.9 us -> 21.2 us
  Pallas kernels: 5.05 us -> 3.65 us
  local copies, waits for them, and re-layouts: 6.46 us -> 7.47 us
    all_to_all x0 -> x1, blocking collectives: none -> 16.5 us  [on_device(): joined = lax.all_to_all(slots, 'tp', 0, 0)]
    all_to_all x1 -> x0, waiting for transfers between devices: 11.7 us -> none  [on_device(): joined = lax.all_to_all(slots, 'tp', 0, 0)]
    all_to_all x1 -> x0, starting transfers between devices: 5.65 us -> none  [on_device(): joined = lax.all_to_all(slots, 'tp', 0, 0)]
    pallas_call x3, Pallas kernels: 5.05 us -> 3.65 us  [call(): pl.pallas_call(kernel, out_shape=out_shape, in_specs=specs, out_specs=tup...]
    dynamic_slice x0 -> x1, local copies, waits for them, and re-layouts: none -> 1.21 us  [on_device(): lax.dynamic_slice_in_dim(cached_key_rows[0], SHARE * side, SHARE, 0)]
    all_to_all x1, waiting for transfers between devices: 7.55 us -> 6.4 us  [on_device(): pieces = lax.all_to_all(copies, 'tp', 0, 0)]
  transfers between devices with their start and end apart: 9 -> 8, of which waited for: 4 -> 3; matrix products, arithmetic and copies ran while one was open for 14% -> 15% of each run, Pallas kernels for 1% -> 0%
where the time goes in v4:
time: 88.3 us; the launch traced here: 87.7 us
  blocking collectives  32 us (36%)
  starting transfers between devices  21.2 us (24%)
  waiting for transfers between devices  15.7 us (18%)
  local copies, waits for them, and re-layouts  7.47 us (8%)
  matrix products  6.03 us (7%)
  Pallas kernels  3.65 us (4%)
  between operations  0.92 us (1%)
    all_to_all x1, blocking collectives, on_device(): joined = lax.all_to_all(slots, 'tp', 0, 0)  16.5 us
    all_to_all x1, blocking collectives, on_device(): arrived = lax.all_to_all(sent, 'tp', 0, 0)  15.5 us
    all_to_all x1, starting transfers between devices, on_device(): pieces = lax.all_to_all(copies, 'tp', 0, 0)  11.4 us
    all_to_all x1, waiting for transfers between devices, on_device(): pieces = lax.all_to_all(copies, 'tp', 0, 0)  6.4 us
    all_to_all x1, starting transfers between devices, on_device(): received = lax.all_to_all(update, 'tp', 0, 0)  5.08 us
    all_to_all x1, waiting for transfers between devices, on_device(): received = lax.all_to_all(update, 'tp', 0, 0)  5.01 us
    ppermute x4, starting transfers between devices, on_device(): given.append(lax.ppermute(part, 'tp', pairs))  4.75 us
    ppermute x2, waiting for transfers between devices, passed_along(): lax.ppermute(array, axis, [(i, (i + by) % devices) for i in range(devices)])  4.32 us
  transfers between devices with their start and end apart: 8, of which 3 were waited for; matrix products, arithmetic and copies ran while one was open for 15% of the time, Pallas kernels for 0%

profile of v4, /device:TPU:32, one launch (start us, length us, event | category | flops | bytes accessed | tf_op | source)
XLA Modules:
  0.0 87.7 jit_solution(7476002514661438289)
XLA Ops:
  0.6 0.0 copy-start
  0.6 0.0 collective-permute-start.2
  0.7 1.6 %broadcast_in_dim.9 = bf16[32,24,256]{2,1,0:T(8,128)(2,1)} broadcast(bf16[24,256]{1,0:T(8,128)(2,1)} %bitcast.49), dimensions={1,2} | broadcast | bytes 405504 | tf_op jit(solution)/shard_map/broadcast_in_dim | solution.py:291
  2.2 11.4 %all-to-all-start = ((bf16[32,24,256]{2,1,0:T(8,128)(2,1)}), bf16[32,24,256]{2,1,0:T(8,128)(2,1)S(1)}, u32[]{:S(2)}, u32[]{:S(2)}) async-start(bf16[32,24,256]{2,1,0:T(8,128)(2,1)} %broadcast_in_dim.9), calls=%async_computation | async-start | bytes 786432 | tf_op jit(solution)/shard_map/all_to_all | solution.py:292
  13.6 0.0 copy-start.2
  13.7 0.0 copy-start.4
  13.7 0.0 copy-start.3
  13.7 2.2 %dynamic-slice_bitcast_fusion.3 = (bf16[6,32,1024]{2,1,0:T(8,128)(2,1)}, bf16[6,32,1024]{2,1,0:T(8,128)(2,1)}) fusion(bf16[1,24,32,1024]{3,2,1,0:T(8,128)(2,1)} %param.14, s32[]{:T(128)S(6)} %select_n.25, s32[]{:T(128)S(6)} %select_n.24), kind=kLoop, calls=%fused_computation.18 | loop fusion | bytes 1572872 | tf_op jit(solution)/shard_map/dynamic_slice | solution.py:287
  15.9 2.7 %collective-permute-start.1 = (bf16[6,32,1024]{2,1,0:T(8,128)(2,1)}, bf16[6,32,1024]{2,1,0:T(8,128)(2,1)S(1)}, u32[]{:S(2)}, u32[]{:S(2)}) collective-permute-start(bf16[6,32,1024]{2,1,0:T(8,128)(2,1)} %get-tuple-element.8), channel_id=1, source_target_pairs={{0,24},{1,25},{2,26},{3,27},{4,28},{5,29},{6,30},{7,31},{8,16},{9,... | collective-permute-start | bytes 1179656 | tf_op jit(solution)/shard_map/ppermute | solution.py:288
  18.6 0.2 collective-permute-start
  18.8 0.0 copy-done.2
  18.8 0.9 %dynamic-slice_bitcast_fusion.1 = (bf16[6,32,1024]{2,1,0:T(8,128)(2,1)}, bf16[6,32,1024]{2,1,0:T(8,128)(2,1)}) fusion(bf16[1,24,32,1024]{3,2,1,0:T(8,128)(2,1)S(1)} %copy-done.2, s32[]{:T(128)S(6)} %select_n.25, s32[]{:T(128)S(6)} %select_n.24), kind=kLoop, calls=%fused_computation.16 | loop fusion | bytes 1572872 | tf_op jit(solution)/shard_map/dynamic_slice | solution.py:287
  19.7 1.2 %collective-permute-start.4 = (bf16[6,32,1024]{2,1,0:T(8,128)(2,1)}, bf16[6,32,1024]{2,1,0:T(8,128)(2,1)}, u32[]{:S(2)}, u32[]{:S(2)}) collective-permute-start(bf16[6,32,1024]{2,1,0:T(8,128)(2,1)} %get-tuple-element.6), channel_id=1, source_target_pairs={{0,24},{1,25},{2,26},{3,27},{4,28},{5,29},{6,30},{7,31},{8,16},{9,... | collective-permute-start | bytes 1179656 | tf_op jit(solution)/shard_map/ppermute | solution.py:288
  20.9 0.7 collective-permute-start.3
  21.6 0.0 copy-done.4
  21.6 0.0 copy-done.3
  21.6 1.2 %dynamic-slice_bitcast_fusion.rest_2_.keys_own = bf16[12,32,1024]{2,1,0:T(8,128)(2,1)S(1)} fusion(bf16[1,24,32,1024]{3,2,1,0:T(8,128)(2,1)} %param.14, s32[]{:T(128)S(6)} %select_n.26), kind=kLoop, calls=%fused_computation.14 | loop fusion | bytes 1572868 | tf_op jit(solution)/shard_map/dynamic_slice | solution.py:290
  22.8 0.2 convert_reduce_fusion
  23.0 0.1 fusion.12.spread_ref
  23.1 6.4 %all-to-all-done = bf16[32,24,256]{2,1,0:T(8,128)(2,1)S(1)} async-done(((bf16[32,24,256]{2,1,0:T(8,128)(2,1)}), bf16[32,24,256]{2,1,0:T(8,128)(2,1)S(1)}, u32[]{:S(2)}, u32[]{:S(2)}) %all-to-all-start) | async-done | bytes 393248 | tf_op jit(solution)/shard_map/all_to_all | solution.py:292
  29.5 0.2 fusion.8
  29.7 0.2 fusion.11
  30.0 1.7 %fusion.5 = bf16[2,64]{1,0:T(2,128)(2,1)S(1)} fusion(bf16[24,8192]{1,0:T(8,128)(2,1)S(1)} %bitcast.45, bf16[1,1,8192,64]{2,3,1,0:T(8,128)(2,1)} %param.12, pred[24]{0:T(512)(128)(4,1)S(1)} %broadcast_compare_fusion, s32[24]{0:T(128)S(1)} %convert_reduce_fusion), kind=kOutput, calls=%fused_computation.7 | convolution fusion | flops 25173728 | bytes 1442168 | tf_op jit(solution)/shard_map/dot_general | solution.py:298
  31.7 0.0 copy-done
  31.7 0.3 fusion
  32.0 0.1 reshape.91
  32.3 0.6 pad.14
  32.9 5.1 %all-to-all-start.1 = ((bf16[32,8,128]{2,1,0:T(8,128)(2,1)}), bf16[32,8,128]{2,1,0:T(8,128)(2,1)S(1)}, u32[]{:S(2)}, u32[]{:S(2)}) async-start(bf16[32,8,128]{2,1,0:T(8,128)(2,1)} %pad.14), calls=%async_computation.1 | async-start | bytes 131072 | tf_op jit(solution)/shard_map/all_to_all | solution.py:306
  38.0 4.0 %fusion.1 = f32[24,320]{1,0:T(8,128)S(1)} fusion(bf16[24,8192]{1,0:T(8,128)(2,1)S(1)} %bitcast.46, bf16[1,8192,320]{1,2,0:T(8,128)(2,1)} %param.11), kind=kOutput, calls=%fused_computation.2 | convolution fusion | flops 125829120 | bytes 5666816 | tf_op jit(solution)/shard_map/dot_general | solution.py:307
  42.0 0.0 copy-start.1
  42.0 0.0 collective-permute-done.2.rest_3_.moved_ref
  42.0 0.0 collective-permute-done.1.rest_1_.keys_b
  42.0 0.0 collective-permute-done.rest_0_.keys_a
  42.0 0.0 collective-permute-done.4.rest_5_.values_b
  42.1 0.0 collective-permute-done.3.rest_4_.values_a
  42.1 5.0 %all-to-all-done.1.received_ref = bf16[32,8,128]{2,1,0:T(8,128)(2,1)S(1)} async-done(((bf16[32,8,128]{2,1,0:T(8,128)(2,1)}), bf16[32,8,128]{2,1,0:T(8,128)(2,1)S(1)}, u32[]{:S(2)}, u32[]{:S(2)}) %all-to-all-start.1) | async-done | bytes 65568 | tf_op jit(solution)/shard_map/all_to_all | solution.py:306
  47.1 0.3 shard_map.104
  47.3 16.5 %all_to_all.20.slots_ref = bf16[32,32,128]{2,1,0:T(8,128)(2,1)S(1)} all-to-all(bf16[32,32,128]{2,1,0:T(8,128)(2,1)S(1)} %shard_map.104), channel_id=1, replica_groups=mesh['section'=8,'tp'=32] {'tp'}, dimensions={0} | all-to-all | bytes 524288 | tf_op jit(solution)/shard_map/all_to_all | solution.py:320
  63.8 0.0 copy-done.1
  63.8 2.9 %shard_map.105 = (bf16[32,32,128]{2,1,0:T(8,128)(2,1)S(1)}, bf16[24,256]{1,0:T(8,128)(2,1)}) custom-call(bf16[32,32,128]{2,1,0:T(8,128)(2,1)S(1)} %all_to_all.20.slots_ref, s32[24]{0:T(128)S(1)} %bitcast.43, bf16[12,32,1024]{2,1,0:T(8,128)(2,1)S(1)} %dynamic-slice_bitcast_fusion.rest_2_.keys_own, bf16[24,32,1024]{2,1,0:T(8,128)(2,1)} %bitcast.44, ...), custom_call_target="tpu_custom_call" | custom-call | tf_op jit(solution)/shard_map/pallas_call | solution.py:48
  66.7 15.5 %all_to_all.21.arrived_ref = bf16[32,32,128]{2,1,0:T(8,128)(2,1)S(1)} all-to-all(bf16[32,32,128]{2,1,0:T(8,128)(2,1)S(1)} %get-tuple-element.5), channel_id=1, replica_groups=mesh['section'=8,'tp'=32] {'tp'}, dimensions={0} | all-to-all | bytes 524288 | tf_op jit(solution)/shard_map/all_to_all | solution.py:347
  82.3 0.5 shard_map.106
  82.8 0.0 collective-permute-start.5
  82.8 4.3 %collective-permute-done.5 = bf16[24,256]{1,0:T(8,128)(2,1)S(1)} collective-permute-done((bf16[24,256]{1,0:T(8,128)(2,1)S(1)}, bf16[24,256]{1,0:T(8,128)(2,1)S(1)}, u32[]{:S(2)}, u32[]{:S(2)}) %collective-permute-start.5) | collective-permute-done | bytes 12320 | tf_op jit(solution)/shard_map/ppermute | solution.py:36
  87.1 0.6 copy.21
  (12 shorter events, 0.2 us)
Async XLA Ops:
  0.6 31.1 %copy-start = (bf16[1,1,64,10240]{3,2,1,0:T(8,128)(2,1)S(1)}, bf16[1,1,64,10240]{3,2,1,0:T(8,128)(2,1)}, u32[]{:S(2)}) copy-start(bf16[1,1,64,10240]{3,2,1,0:T(8,128)(2,1)} %param.13) | copy-start | bytes 3932164
  0.6 41.4 %collective-permute-start.2 = (bf16[24,256]{1,0:T(8,128)(2,1)}, bf16[24,256]{1,0:T(8,128)(2,1)S(1)}, u32[]{:S(2)}, u32[]{:S(2)}) collective-permute-start(bf16[24,256]{1,0:T(8,128)(2,1)} %bitcast.48), channel_id=1, source_target_pairs={{0,32},{32,64},{64,96},{96,128},{128,160},{160,192},{192,224},{224... | collective-permute-start | bytes 36872 | tf_op jit(solution)/shard_map/ppermute | solution.py:36
  2.2 27.3 %all-to-all-start = ((bf16[32,24,256]{2,1,0:T(8,128)(2,1)}), bf16[32,24,256]{2,1,0:T(8,128)(2,1)S(1)}, u32[]{:S(2)}, u32[]{:S(2)}) async-start(bf16[32,24,256]{2,1,0:T(8,128)(2,1)} %broadcast_in_dim.9), calls=%async_computation | async-start | bytes 786432 | tf_op jit(solution)/shard_map/all_to_all | solution.py:292
  13.6 5.2 %copy-start.2 = (bf16[1,24,32,1024]{3,2,1,0:T(8,128)(2,1)S(1)}, bf16[1,24,32,1024]{3,2,1,0:T(8,128)(2,1)}, u32[]{:S(2)}) copy-start(bf16[1,24,32,1024]{3,2,1,0:T(8,128)(2,1)} %param.15) | copy-start | bytes 4718596
  13.7 7.9 %copy-start.4 = (s32[1,24,1]{1,2,0:T(1,128)S(1)}, s32[1,24,1]{1,2,0:T(1,128)}, u32[]{:S(2)}) copy-start(s32[1,24,1]{1,2,0:T(1,128)} %param.16) | copy-start | bytes 292
  13.7 7.9 %copy-start.3 = (f32[8192]{0:T(1024)S(1)}, f32[8192]{0:T(1024)}, u32[]{:S(2)}) copy-start(f32[8192]{0:T(1024)} %param.10) | copy-start | bytes 98308
  15.9 26.2 %collective-permute-start.1 = (bf16[6,32,1024]{2,1,0:T(8,128)(2,1)}, bf16[6,32,1024]{2,1,0:T(8,128)(2,1)S(1)}, u32[]{:S(2)}, u32[]{:S(2)}) collective-permute-start(bf16[6,32,1024]{2,1,0:T(8,128)(2,1)} %get-tuple-element.8), channel_id=1, source_target_pairs={{0,24},{1,25},{2,26},{3,27},{4,28},{5,29},{6,30},{7,31},{8,16},{9,... | collective-permute-start | bytes 1179656 | tf_op jit(solution)/shard_map/ppermute | solution.py:288
  18.6 23.4 %collective-permute-start = (bf16[6,32,1024]{2,1,0:T(8,128)(2,1)}, bf16[6,32,1024]{2,1,0:T(8,128)(2,1)S(1)}, u32[]{:S(2)}, u32[]{:S(2)}) collective-permute-start(bf16[6,32,1024]{2,1,0:T(8,128)(2,1)} %get-tuple-element.9), channel_id=1, source_target_pairs={{0,8},{1,9},{2,10},{3,11},{4,12},{5,13},{6,14},{7,15},{8,0},{9,1},... | collective-permute-start | bytes 1179656 | tf_op jit(solution)/shard_map/ppermute | solution.py:288
  19.7 22.3 %collective-permute-start.4 = (bf16[6,32,1024]{2,1,0:T(8,128)(2,1)}, bf16[6,32,1024]{2,1,0:T(8,128)(2,1)}, u32[]{:S(2)}, u32[]{:S(2)}) collective-permute-start(bf16[6,32,1024]{2,1,0:T(8,128)(2,1)} %get-tuple-element.6), channel_id=1, source_target_pairs={{0,24},{1,25},{2,26},{3,27},{4,28},{5,29},{6,30},{7,31},{8,16},{9,... | collective-permute-start | bytes 1179656 | tf_op jit(solution)/shard_map/ppermute | solution.py:288
  20.9 21.1 %collective-permute-start.3 = (bf16[6,32,1024]{2,1,0:T(8,128)(2,1)}, bf16[6,32,1024]{2,1,0:T(8,128)(2,1)}, u32[]{:S(2)}, u32[]{:S(2)}) collective-permute-start(bf16[6,32,1024]{2,1,0:T(8,128)(2,1)} %get-tuple-element.7), channel_id=1, source_target_pairs={{0,8},{1,9},{2,10},{3,11},{4,12},{5,13},{6,14},{7,15},{8,0},{9,1},... | collective-permute-start | bytes 1179656 | tf_op jit(solution)/shard_map/ppermute | solution.py:288
  32.9 14.2 %all-to-all-start.1 = ((bf16[32,8,128]{2,1,0:T(8,128)(2,1)}), bf16[32,8,128]{2,1,0:T(8,128)(2,1)S(1)}, u32[]{:S(2)}, u32[]{:S(2)}) async-start(bf16[32,8,128]{2,1,0:T(8,128)(2,1)} %pad.14), calls=%async_computation.1 | async-start | bytes 131072 | tf_op jit(solution)/shard_map/all_to_all | solution.py:306
  42.0 21.8 %copy-start.1 = (s32[1,24]{1,0:T(1,128)S(1)}, s32[1,24]{1,0:T(1,128)}, u32[]{:S(2)}) copy-start(s32[1,24]{1,0:T(1,128)} %param.17) | copy-start | bytes 292
  82.8 4.3 %collective-permute-start.5 = (bf16[24,256]{1,0:T(8,128)(2,1)S(1)}, bf16[24,256]{1,0:T(8,128)(2,1)S(1)}, u32[]{:S(2)}, u32[]{:S(2)}) collective-permute-start(bf16[24,256]{1,0:T(8,128)(2,1)S(1)} %convert_element_type.55), channel_id=1, source_target_pairs={{0,32},{32,64},{64,96},{96,128},{128,160},{160,192},{192,224},{224... | collective-permute-start | bytes 36872 | tf_op jit(solution)/shard_map/ppermute | solution.py:36

commit v5 on v4

--- a/solution.py
+++ b/solution.py
@@ -129,7 +129,8 @@
     for block in range(2):
         for row in range(SHARE):
             start = (device, first_giver if row < GIVEN else second_giver)[block] * SPAN
-            seen = (position < used_ref[SHARE * side + row] - start) & (row_lane == row % QUAD)
+            used = jnp.where(side == 0, used_ref[:, row : row + 1], used_ref[:, SHARE + row : SHARE + row + 1])
+            seen = (position < used - start) & (row_lane == row % QUAD)
             to = SPAN * (QUAD * block + row % QUAD)
             biases[row // QUAD, to : to + SPAN, :] = jnp.where(seen, 0.0, NEGATIVE)
     low = low_lanes((8, HD))
@@ -337,7 +338,7 @@
             pltpu.SemaphoreType.DMA,
         ],
         joined,
-        Far(lengths[0], pltpu.SMEM),
+        lengths,
         own_keys,
         Far(cached_value_rows[0]),
         *given[:2],

time: 88.3 us -> 88 us (level)
  no operation moved by 1% of the time
where the time goes in v5:
time: 88 us; the launch traced here: 87.5 us
  blocking collectives  32 us (36%)
  starting transfers between devices  21.2 us (24%)
  waiting for transfers between devices  15.7 us (18%)
  local copies, waits for them, and re-layouts  7.47 us (8%)
  matrix products  6.03 us (7%)
  Pallas kernels  3.4 us (4%)
  between operations  0.92 us (1%)
    all_to_all x1, blocking collectives, on_device(): joined = lax.all_to_all(slots, 'tp', 0, 0)  16.5 us
    all_to_all x1, blocking collectives, on_device(): arrived = lax.all_to_all(sent, 'tp', 0, 0)  15.5 us
    all_to_all x1, starting transfers between devices, on_device(): pieces = lax.all_to_all(copies, 'tp', 0, 0)  11.4 us
    all_to_all x1, waiting for transfers between devices, on_device(): pieces = lax.all_to_all(copies, 'tp', 0, 0)  6.4 us
    all_to_all x1, starting transfers between devices, on_device(): received = lax.all_to_all(update, 'tp', 0, 0)  5.08 us
    all_to_all x1, waiting for transfers between devices, on_device(): received = lax.all_to_all(update, 'tp', 0, 0)  5.01 us
    ppermute x4, starting transfers between devices, on_device(): given.append(lax.ppermute(part, 'tp', pairs))  4.75 us
    ppermute x2, waiting for transfers between devices, passed_along(): lax.ppermute(array, axis, [(i, (i + by) % devices) for i in range(devices)])  4.32 us
  transfers between devices with their start and end apart: 8, of which 3 were waited for; matrix products, arithmetic and copies ran while one was open for 15% of the time, Pallas kernels for 0%

profile of v5, /device:TPU:32, one launch (start us, length us, event | category | flops | bytes accessed | tf_op | source)
XLA Modules:
  0.0 87.5 jit_solution(16312714454676973756)
XLA Ops:
  0.6 0.0 copy-start
  0.6 0.0 collective-permute-start.2
  0.7 1.6 %broadcast_in_dim.9 = bf16[32,24,256]{2,1,0:T(8,128)(2,1)} broadcast(bf16[24,256]{1,0:T(8,128)(2,1)} %bitcast.47), dimensions={1,2} | broadcast | bytes 405504 | tf_op jit(solution)/shard_map/broadcast_in_dim | solution.py:292
  2.2 11.4 %all-to-all-start = ((bf16[32,24,256]{2,1,0:T(8,128)(2,1)}), bf16[32,24,256]{2,1,0:T(8,128)(2,1)S(1)}, u32[]{:S(2)}, u32[]{:S(2)}) async-start(bf16[32,24,256]{2,1,0:T(8,128)(2,1)} %broadcast_in_dim.9), calls=%async_computation | async-start | bytes 786432 | tf_op jit(solution)/shard_map/all_to_all | solution.py:293
  13.6 0.0 copy-start.2
  13.7 0.0 copy-start.4
  13.7 0.0 copy-start.3
  13.7 2.2 %dynamic-slice_bitcast_fusion.3 = (bf16[6,32,1024]{2,1,0:T(8,128)(2,1)}, bf16[6,32,1024]{2,1,0:T(8,128)(2,1)}) fusion(bf16[1,24,32,1024]{3,2,1,0:T(8,128)(2,1)} %param.14, s32[]{:T(128)S(6)} %select_n.25, s32[]{:T(128)S(6)} %select_n.24), kind=kLoop, calls=%fused_computation.18 | loop fusion | bytes 1572872 | tf_op jit(solution)/shard_map/dynamic_slice | solution.py:288
  15.9 2.7 %collective-permute-start.1 = (bf16[6,32,1024]{2,1,0:T(8,128)(2,1)}, bf16[6,32,1024]{2,1,0:T(8,128)(2,1)S(1)}, u32[]{:S(2)}, u32[]{:S(2)}) collective-permute-start(bf16[6,32,1024]{2,1,0:T(8,128)(2,1)} %get-tuple-element.8), channel_id=1, source_target_pairs={{0,24},{1,25},{2,26},{3,27},{4,28},{5,29},{6,30},{7,31},{8,16},{9,... | collective-permute-start | bytes 1179656 | tf_op jit(solution)/shard_map/ppermute | solution.py:289
  18.6 0.2 collective-permute-start
  18.8 0.0 copy-done.2
  18.8 0.9 %dynamic-slice_bitcast_fusion.1 = (bf16[6,32,1024]{2,1,0:T(8,128)(2,1)}, bf16[6,32,1024]{2,1,0:T(8,128)(2,1)}) fusion(bf16[1,24,32,1024]{3,2,1,0:T(8,128)(2,1)S(1)} %copy-done.2, s32[]{:T(128)S(6)} %select_n.25, s32[]{:T(128)S(6)} %select_n.24), kind=kLoop, calls=%fused_computation.16 | loop fusion | bytes 1572872 | tf_op jit(solution)/shard_map/dynamic_slice | solution.py:288
  19.7 1.2 %collective-permute-start.4 = (bf16[6,32,1024]{2,1,0:T(8,128)(2,1)}, bf16[6,32,1024]{2,1,0:T(8,128)(2,1)}, u32[]{:S(2)}, u32[]{:S(2)}) collective-permute-start(bf16[6,32,1024]{2,1,0:T(8,128)(2,1)} %get-tuple-element.6), channel_id=1, source_target_pairs={{0,24},{1,25},{2,26},{3,27},{4,28},{5,29},{6,30},{7,31},{8,16},{9,... | collective-permute-start | bytes 1179656 | tf_op jit(solution)/shard_map/ppermute | solution.py:289
  20.9 0.7 collective-permute-start.3
  21.6 0.0 copy-done.4
  21.6 0.0 copy-done.3
  21.6 1.2 %dynamic-slice_bitcast_fusion.rest_2_.keys_own = bf16[12,32,1024]{2,1,0:T(8,128)(2,1)S(1)} fusion(bf16[1,24,32,1024]{3,2,1,0:T(8,128)(2,1)} %param.14, s32[]{:T(128)S(6)} %select_n.26), kind=kLoop, calls=%fused_computation.14 | loop fusion | bytes 1572868 | tf_op jit(solution)/shard_map/dynamic_slice | solution.py:291
  22.8 0.2 convert_reduce_fusion
  23.0 0.1 fusion.12.spread_ref
  23.1 6.4 %all-to-all-done = bf16[32,24,256]{2,1,0:T(8,128)(2,1)S(1)} async-done(((bf16[32,24,256]{2,1,0:T(8,128)(2,1)}), bf16[32,24,256]{2,1,0:T(8,128)(2,1)S(1)}, u32[]{:S(2)}, u32[]{:S(2)}) %all-to-all-start) | async-done | bytes 393248 | tf_op jit(solution)/shard_map/all_to_all | solution.py:293
  29.5 0.2 fusion.8
  29.7 0.2 fusion.11
  30.0 1.7 %fusion.5 = bf16[2,64]{1,0:T(2,128)(2,1)S(1)} fusion(bf16[24,8192]{1,0:T(8,128)(2,1)S(1)} %bitcast.43, bf16[1,1,8192,64]{2,3,1,0:T(8,128)(2,1)} %param.12, pred[24]{0:T(512)(128)(4,1)S(1)} %broadcast_compare_fusion, s32[24]{0:T(128)S(1)} %convert_reduce_fusion), kind=kOutput, calls=%fused_computation.7 | convolution fusion | flops 25173728 | bytes 1442168 | tf_op jit(solution)/shard_map/dot_general | solution.py:299
  31.7 0.0 copy-done
  31.7 0.3 fusion
  32.0 0.1 reshape.91
  32.3 0.6 pad.14
  32.9 5.1 %all-to-all-start.1 = ((bf16[32,8,128]{2,1,0:T(8,128)(2,1)}), bf16[32,8,128]{2,1,0:T(8,128)(2,1)S(1)}, u32[]{:S(2)}, u32[]{:S(2)}) async-start(bf16[32,8,128]{2,1,0:T(8,128)(2,1)} %pad.14), calls=%async_computation.1 | async-start | bytes 131072 | tf_op jit(solution)/shard_map/all_to_all | solution.py:307
  38.0 4.0 %fusion.1 = f32[24,320]{1,0:T(8,128)S(1)} fusion(bf16[24,8192]{1,0:T(8,128)(2,1)S(1)} %bitcast.44, bf16[1,8192,320]{1,2,0:T(8,128)(2,1)} %param.11), kind=kOutput, calls=%fused_computation.2 | convolution fusion | flops 125829120 | bytes 5666816 | tf_op jit(solution)/shard_map/dot_general | solution.py:308
  42.0 0.0 copy-start.1
  42.0 0.0 collective-permute-done.2.rest_3_.moved_ref
  42.0 0.0 collective-permute-done.1.rest_1_.keys_b
  42.0 0.0 collective-permute-done.rest_0_.keys_a
  42.0 0.0 collective-permute-done.4.rest_5_.values_b
  42.1 0.0 collective-permute-done.3.rest_4_.values_a
  42.1 5.0 %all-to-all-done.1.received_ref = bf16[32,8,128]{2,1,0:T(8,128)(2,1)S(1)} async-done(((bf16[32,8,128]{2,1,0:T(8,128)(2,1)}), bf16[32,8,128]{2,1,0:T(8,128)(2,1)S(1)}, u32[]{:S(2)}, u32[]{:S(2)}) %all-to-all-start.1) | async-done | bytes 65568 | tf_op jit(solution)/shard_map/all_to_all | solution.py:307
  47.1 0.3 shard_map.104
  47.3 16.5 %all_to_all.20.slots_ref = bf16[32,32,128]{2,1,0:T(8,128)(2,1)S(1)} all-to-all(bf16[32,32,128]{2,1,0:T(8,128)(2,1)S(1)} %shard_map.104), channel_id=1, replica_groups=mesh['section'=8,'tp'=32] {'tp'}, dimensions={0} | all-to-all | bytes 524288 | tf_op jit(solution)/shard_map/all_to_all | solution.py:321
  63.8 0.0 copy-done.1
  63.8 2.6 %shard_map.105 = (bf16[32,32,128]{2,1,0:T(8,128)(2,1)S(1)}, bf16[24,256]{1,0:T(8,128)(2,1)}) custom-call(bf16[32,32,128]{2,1,0:T(8,128)(2,1)S(1)} %all_to_all.20.slots_ref, s32[1,24]{1,0:T(1,128)S(1)} %copy-done.1, bf16[12,32,1024]{2,1,0:T(8,128)(2,1)S(1)} %dynamic-slice_bitcast_fusion.rest_2_.keys_own, bf16[24,32,1024]{2,1,0:T(8,128)(2,1)} %bitcast.42, ...), custom_call_target="tpu_custom_call" | custom-call | tf_op jit(solution)/shard_map/pallas_call | solution.py:48
  66.5 15.5 %all_to_all.21.arrived_ref = bf16[32,32,128]{2,1,0:T(8,128)(2,1)S(1)} all-to-all(bf16[32,32,128]{2,1,0:T(8,128)(2,1)S(1)} %get-tuple-element.5), channel_id=1, replica_groups=mesh['section'=8,'tp'=32] {'tp'}, dimensions={0} | all-to-all | bytes 524288 | tf_op jit(solution)/shard_map/all_to_all | solution.py:348
  82.0 0.5 shard_map.106
  82.5 0.0 collective-permute-start.5
  82.6 4.3 %collective-permute-done.5 = bf16[24,256]{1,0:T(8,128)(2,1)S(1)} collective-permute-done((bf16[24,256]{1,0:T(8,128)(2,1)S(1)}, bf16[24,256]{1,0:T(8,128)(2,1)S(1)}, u32[]{:S(2)}, u32[]{:S(2)}) %collective-permute-start.5) | collective-permute-done | bytes 12320 | tf_op jit(solution)/shard_map/ppermute | solution.py:36
  86.9 0.6 copy.21
  (12 shorter events, 0.2 us)
Async XLA Ops:
  0.6 31.1 %copy-start = (bf16[1,1,64,10240]{3,2,1,0:T(8,128)(2,1)S(1)}, bf16[1,1,64,10240]{3,2,1,0:T(8,128)(2,1)}, u32[]{:S(2)}) copy-start(bf16[1,1,64,10240]{3,2,1,0:T(8,128)(2,1)} %param.13) | copy-start | bytes 3932164
  0.6 41.4 %collective-permute-start.2 = (bf16[24,256]{1,0:T(8,128)(2,1)}, bf16[24,256]{1,0:T(8,128)(2,1)S(1)}, u32[]{:S(2)}, u32[]{:S(2)}) collective-permute-start(bf16[24,256]{1,0:T(8,128)(2,1)} %bitcast.46), channel_id=1, source_target_pairs={{0,32},{32,64},{64,96},{96,128},{128,160},{160,192},{192,224},{224... | collective-permute-start | bytes 36872 | tf_op jit(solution)/shard_map/ppermute | solution.py:36
  2.2 27.3 %all-to-all-start = ((bf16[32,24,256]{2,1,0:T(8,128)(2,1)}), bf16[32,24,256]{2,1,0:T(8,128)(2,1)S(1)}, u32[]{:S(2)}, u32[]{:S(2)}) async-start(bf16[32,24,256]{2,1,0:T(8,128)(2,1)} %broadcast_in_dim.9), calls=%async_computation | async-start | bytes 786432 | tf_op jit(solution)/shard_map/all_to_all | solution.py:293
  13.6 5.2 %copy-start.2 = (bf16[1,24,32,1024]{3,2,1,0:T(8,128)(2,1)S(1)}, bf16[1,24,32,1024]{3,2,1,0:T(8,128)(2,1)}, u32[]{:S(2)}) copy-start(bf16[1,24,32,1024]{3,2,1,0:T(8,128)(2,1)} %param.15) | copy-start | bytes 4718596
  13.7 7.9 %copy-start.4 = (s32[1,24,1]{1,2,0:T(1,128)S(1)}, s32[1,24,1]{1,2,0:T(1,128)}, u32[]{:S(2)}) copy-start(s32[1,24,1]{1,2,0:T(1,128)} %param.16) | copy-start | bytes 292
  13.7 7.9 %copy-start.3 = (f32[8192]{0:T(1024)S(1)}, f32[8192]{0:T(1024)}, u32[]{:S(2)}) copy-start(f32[8192]{0:T(1024)} %param.10) | copy-start | bytes 98308
  15.9 26.2 %collective-permute-start.1 = (bf16[6,32,1024]{2,1,0:T(8,128)(2,1)}, bf16[6,32,1024]{2,1,0:T(8,128)(2,1)S(1)}, u32[]{:S(2)}, u32[]{:S(2)}) collective-permute-start(bf16[6,32,1024]{2,1,0:T(8,128)(2,1)} %get-tuple-element.8), channel_id=1, source_target_pairs={{0,24},{1,25},{2,26},{3,27},{4,28},{5,29},{6,30},{7,31},{8,16},{9,... | collective-permute-start | bytes 1179656 | tf_op jit(solution)/shard_map/ppermute | solution.py:289
  18.6 23.4 %collective-permute-start = (bf16[6,32,1024]{2,1,0:T(8,128)(2,1)}, bf16[6,32,1024]{2,1,0:T(8,128)(2,1)S(1)}, u32[]{:S(2)}, u32[]{:S(2)}) collective-permute-start(bf16[6,32,1024]{2,1,0:T(8,128)(2,1)} %get-tuple-element.9), channel_id=1, source_target_pairs={{0,8},{1,9},{2,10},{3,11},{4,12},{5,13},{6,14},{7,15},{8,0},{9,1},... | collective-permute-start | bytes 1179656 | tf_op jit(solution)/shard_map/ppermute | solution.py:289
  19.7 22.3 %collective-permute-start.4 = (bf16[6,32,1024]{2,1,0:T(8,128)(2,1)}, bf16[6,32,1024]{2,1,0:T(8,128)(2,1)}, u32[]{:S(2)}, u32[]{:S(2)}) collective-permute-start(bf16[6,32,1024]{2,1,0:T(8,128)(2,1)} %get-tuple-element.6), channel_id=1, source_target_pairs={{0,24},{1,25},{2,26},{3,27},{4,28},{5,29},{6,30},{7,31},{8,16},{9,... | collective-permute-start | bytes 1179656 | tf_op jit(solution)/shard_map/ppermute | solution.py:289
  20.9 21.1 %collective-permute-start.3 = (bf16[6,32,1024]{2,1,0:T(8,128)(2,1)}, bf16[6,32,1024]{2,1,0:T(8,128)(2,1)}, u32[]{:S(2)}, u32[]{:S(2)}) collective-permute-start(bf16[6,32,1024]{2,1,0:T(8,128)(2,1)} %get-tuple-element.7), channel_id=1, source_target_pairs={{0,8},{1,9},{2,10},{3,11},{4,12},{5,13},{6,14},{7,15},{8,0},{9,1},... | collective-permute-start | bytes 1179656 | tf_op jit(solution)/shard_map/ppermute | solution.py:289
  32.9 14.2 %all-to-all-start.1 = ((bf16[32,8,128]{2,1,0:T(8,128)(2,1)}), bf16[32,8,128]{2,1,0:T(8,128)(2,1)S(1)}, u32[]{:S(2)}, u32[]{:S(2)}) async-start(bf16[32,8,128]{2,1,0:T(8,128)(2,1)} %pad.14), calls=%async_computation.1 | async-start | bytes 131072 | tf_op jit(solution)/shard_map/all_to_all | solution.py:307
  42.0 21.8 %copy-start.1 = (s32[1,24]{1,0:T(1,128)S(1)}, s32[1,24]{1,0:T(1,128)}, u32[]{:S(2)}) copy-start(s32[1,24]{1,0:T(1,128)} %used_ref.1) | copy-start | bytes 292
  82.5 4.3 %collective-permute-start.5 = (bf16[24,256]{1,0:T(8,128)(2,1)S(1)}, bf16[24,256]{1,0:T(8,128)(2,1)S(1)}, u32[]{:S(2)}, u32[]{:S(2)}) collective-permute-start(bf16[24,256]{1,0:T(8,128)(2,1)S(1)} %convert_element_type.55), channel_id=1, source_target_pairs={{0,32},{32,64},{64,96},{96,128},{128,160},{160,192},{192,224},{224... | collective-permute-start | bytes 36872 | tf_op jit(solution)/shard_map/ppermute | solution.py:36

commit v6 on v5

--- a/solution.py
+++ b/solution.py
@@ -197,14 +197,18 @@
         value = fresh[KVH + at // (TP // KVH)]
         terms = [columns[0:8, q : q + 1] * value[8 * q : 8 * q + 8] for q in range(QUADS)]
         own_terms.append(jnp.concatenate(terms, axis=0))
-    for load in loads:
-        load.wait()
     for gg in range(2):
         level = levels[gg]
         high = level.astype(jnp.bfloat16).astype(jnp.float32)
         middle = (level - high).astype(jnp.bfloat16).astype(jnp.float32)
         rest = pltpu.roll(level - high - middle, 16, 1)
         middle = pltpu.roll(middle, 8, 1)
+        for j in range(16):
+            lines = jnp.where(eighth == j, high, jnp.where(eighth == (j + 1) % 16, middle, rest))
+            result[16 * gg + j, LINES:PART, :] = lines
+    for load in loads:
+        load.wait()
+    for gg in range(2):
         for q in range(QUADS):
             for i in range(4):
                 g = 4 * gg + i
@@ -213,12 +217,11 @@
                 for j in range(4):
                     result[4 * g + j, 8 * q : 8 * q + 8, :] = mixed[8 * j : 8 * j + 8]
         for j in range(16):
-            lines = jnp.where(eighth == j, high, jnp.where(eighth == (j + 1) % 16, middle, rest))
             t = 16 * gg + j
-            whole = result[t]
+            whole = result[t, 0:LINES]
             for at, terms in zip(own_devices, own_terms):
                 whole = whole + jnp.where(at == t, terms, 0.0)
-            sent_ref[t] = jnp.concatenate([whole, lines], axis=0).astype(jnp.bfloat16)
+            sent_ref[t] = jnp.concatenate([whole, result[t, LINES:PART]], axis=0).astype(jnp.bfloat16)
     keep.wait()
 
 
@@ -327,7 +330,7 @@
         [
             pltpu.VMEM((TP, LINES, HD), jnp.float32),
             pltpu.VMEM((2 * KVH, LINES, HD), jnp.float32),
-            pltpu.VMEM((TP, LINES, HD), jnp.float32),
+            pltpu.VMEM((TP, PART, HD), jnp.float32),
             pltpu.VMEM((2, 8, HD), jnp.float32),
             pltpu.VMEM((8, HD), jnp.float32),
             pltpu.VMEM((QUADS, 2 * QUAD * SPAN, HD), jnp.float32),

time: 88 us -> 88 us (level)
  no operation moved by 1% of the time
where the time goes in v6:
time: 88 us; the launch traced here: 87.5 us
  blocking collectives  32 us (36%)
  starting transfers between devices  21.2 us (24%)
  waiting for transfers between devices  15.7 us (18%)
  local copies, waits for them, and re-layouts  7.47 us (8%)
  matrix products  6.03 us (7%)
  Pallas kernels  3.42 us (4%)
  between operations  0.92 us (1%)
    all_to_all x1, blocking collectives, on_device(): joined = lax.all_to_all(slots, 'tp', 0, 0)  16.5 us
    all_to_all x1, blocking collectives, on_device(): arrived = lax.all_to_all(sent, 'tp', 0, 0)  15.5 us
    all_to_all x1, starting transfers between devices, on_device(): pieces = lax.all_to_all(copies, 'tp', 0, 0)  11.4 us
    all_to_all x1, waiting for transfers between devices, on_device(): pieces = lax.all_to_all(copies, 'tp', 0, 0)  6.4 us
    all_to_all x1, starting transfers between devices, on_device(): received = lax.all_to_all(update, 'tp', 0, 0)  5.08 us
    all_to_all x1, waiting for transfers between devices, on_device(): received = lax.all_to_all(update, 'tp', 0, 0)  5.01 us
    ppermute x4, starting transfers between devices, on_device(): given.append(lax.ppermute(part, 'tp', pairs))  4.75 us
    ppermute x2, waiting for transfers between devices, passed_along(): lax.ppermute(array, axis, [(i, (i + by) % devices) for i in range(devices)])  4.32 us
  transfers between devices with their start and end apart: 8, of which 3 were waited for; matrix products, arithmetic and copies ran while one was open for 15% of the time, Pallas kernels for 0%

profile of v6, /device:TPU:32, one launch (start us, length us, event | category | flops | bytes accessed | tf_op | source)
XLA Modules:
  0.0 87.5 jit_solution(630685529695234324)
XLA Ops:
  0.6 0.0 copy-start
  0.6 0.0 collective-permute-start.2
  0.7 1.6 %broadcast_in_dim.9 = bf16[32,24,256]{2,1,0:T(8,128)(2,1)} broadcast(bf16[24,256]{1,0:T(8,128)(2,1)} %bitcast.47), dimensions={1,2} | broadcast | bytes 405504 | tf_op jit(solution)/shard_map/broadcast_in_dim | solution.py:295
  2.2 11.4 %all-to-all-start = ((bf16[32,24,256]{2,1,0:T(8,128)(2,1)}), bf16[32,24,256]{2,1,0:T(8,128)(2,1)S(1)}, u32[]{:S(2)}, u32[]{:S(2)}) async-start(bf16[32,24,256]{2,1,0:T(8,128)(2,1)} %broadcast_in_dim.9), calls=%async_computation | async-start | bytes 786432 | tf_op jit(solution)/shard_map/all_to_all | solution.py:296
  13.6 0.0 copy-start.2
  13.7 0.0 copy-start.4
  13.7 0.0 copy-start.3
  13.7 2.2 %dynamic-slice_bitcast_fusion.3 = (bf16[6,32,1024]{2,1,0:T(8,128)(2,1)}, bf16[6,32,1024]{2,1,0:T(8,128)(2,1)}) fusion(bf16[1,24,32,1024]{3,2,1,0:T(8,128)(2,1)} %param.14, s32[]{:T(128)S(6)} %select_n.25, s32[]{:T(128)S(6)} %select_n.24), kind=kLoop, calls=%fused_computation.18 | loop fusion | bytes 1572872 | tf_op jit(solution)/shard_map/dynamic_slice | solution.py:291
  15.9 2.7 %collective-permute-start.1 = (bf16[6,32,1024]{2,1,0:T(8,128)(2,1)}, bf16[6,32,1024]{2,1,0:T(8,128)(2,1)S(1)}, u32[]{:S(2)}, u32[]{:S(2)}) collective-permute-start(bf16[6,32,1024]{2,1,0:T(8,128)(2,1)} %get-tuple-element.8), channel_id=1, source_target_pairs={{0,24},{1,25},{2,26},{3,27},{4,28},{5,29},{6,30},{7,31},{8,16},{9,... | collective-permute-start | bytes 1179656 | tf_op jit(solution)/shard_map/ppermute | solution.py:292
  18.6 0.2 collective-permute-start
  18.8 0.0 copy-done.2
  18.8 0.9 %dynamic-slice_bitcast_fusion.1 = (bf16[6,32,1024]{2,1,0:T(8,128)(2,1)}, bf16[6,32,1024]{2,1,0:T(8,128)(2,1)}) fusion(bf16[1,24,32,1024]{3,2,1,0:T(8,128)(2,1)S(1)} %copy-done.2, s32[]{:T(128)S(6)} %select_n.25, s32[]{:T(128)S(6)} %select_n.24), kind=kLoop, calls=%fused_computation.16 | loop fusion | bytes 1572872 | tf_op jit(solution)/shard_map/dynamic_slice | solution.py:291
  19.7 1.2 %collective-permute-start.4 = (bf16[6,32,1024]{2,1,0:T(8,128)(2,1)}, bf16[6,32,1024]{2,1,0:T(8,128)(2,1)}, u32[]{:S(2)}, u32[]{:S(2)}) collective-permute-start(bf16[6,32,1024]{2,1,0:T(8,128)(2,1)} %get-tuple-element.6), channel_id=1, source_target_pairs={{0,24},{1,25},{2,26},{3,27},{4,28},{5,29},{6,30},{7,31},{8,16},{9,... | collective-permute-start | bytes 1179656 | tf_op jit(solution)/shard_map/ppermute | solution.py:292
  20.9 0.7 collective-permute-start.3
  21.6 0.0 copy-done.4
  21.6 0.0 copy-done.3
  21.6 1.2 %dynamic-slice_bitcast_fusion.rest_2_.keys_own = bf16[12,32,1024]{2,1,0:T(8,128)(2,1)S(1)} fusion(bf16[1,24,32,1024]{3,2,1,0:T(8,128)(2,1)} %param.14, s32[]{:T(128)S(6)} %select_n.26), kind=kLoop, calls=%fused_computation.14 | loop fusion | bytes 1572868 | tf_op jit(solution)/shard_map/dynamic_slice | solution.py:294
  22.8 0.2 convert_reduce_fusion
  23.0 0.1 fusion.12.spread_ref
  23.1 6.4 %all-to-all-done = bf16[32,24,256]{2,1,0:T(8,128)(2,1)S(1)} async-done(((bf16[32,24,256]{2,1,0:T(8,128)(2,1)}), bf16[32,24,256]{2,1,0:T(8,128)(2,1)S(1)}, u32[]{:S(2)}, u32[]{:S(2)}) %all-to-all-start) | async-done | bytes 393248 | tf_op jit(solution)/shard_map/all_to_all | solution.py:296
  29.5 0.2 fusion.8
  29.7 0.2 fusion.11
  30.0 1.7 %fusion.5 = bf16[2,64]{1,0:T(2,128)(2,1)S(1)} fusion(bf16[24,8192]{1,0:T(8,128)(2,1)S(1)} %bitcast.43, bf16[1,1,8192,64]{2,3,1,0:T(8,128)(2,1)} %param.12, pred[24]{0:T(512)(128)(4,1)S(1)} %broadcast_compare_fusion, s32[24]{0:T(128)S(1)} %convert_reduce_fusion), kind=kOutput, calls=%fused_computation.7 | convolution fusion | flops 25173728 | bytes 1442168 | tf_op jit(solution)/shard_map/dot_general | solution.py:302
  31.7 0.0 copy-done
  31.7 0.3 fusion
  32.0 0.1 reshape.91
  32.3 0.6 pad.14
  32.9 5.1 %all-to-all-start.1 = ((bf16[32,8,128]{2,1,0:T(8,128)(2,1)}), bf16[32,8,128]{2,1,0:T(8,128)(2,1)S(1)}, u32[]{:S(2)}, u32[]{:S(2)}) async-start(bf16[32,8,128]{2,1,0:T(8,128)(2,1)} %pad.14), calls=%async_computation.1 | async-start | bytes 131072 | tf_op jit(solution)/shard_map/all_to_all | solution.py:310
  38.0 4.0 %fusion.1 = f32[24,320]{1,0:T(8,128)S(1)} fusion(bf16[24,8192]{1,0:T(8,128)(2,1)S(1)} %bitcast.44, bf16[1,8192,320]{1,2,0:T(8,128)(2,1)} %param.11), kind=kOutput, calls=%fused_computation.2 | convolution fusion | flops 125829120 | bytes 5666816 | tf_op jit(solution)/shard_map/dot_general | solution.py:311
  42.0 0.0 copy-start.1
  42.0 0.0 collective-permute-done.2.rest_3_.moved_ref
  42.0 0.0 collective-permute-done.1.rest_1_.keys_b
  42.0 0.0 collective-permute-done.rest_0_.keys_a
  42.0 0.0 collective-permute-done.4.rest_5_.values_b
  42.1 0.0 collective-permute-done.3.rest_4_.values_a
  42.1 5.0 %all-to-all-done.1.received_ref = bf16[32,8,128]{2,1,0:T(8,128)(2,1)S(1)} async-done(((bf16[32,8,128]{2,1,0:T(8,128)(2,1)}), bf16[32,8,128]{2,1,0:T(8,128)(2,1)S(1)}, u32[]{:S(2)}, u32[]{:S(2)}) %all-to-all-start.1) | async-done | bytes 65568 | tf_op jit(solution)/shard_map/all_to_all | solution.py:310
  47.1 0.3 shard_map.104
  47.3 16.5 %all_to_all.20.slots_ref = bf16[32,32,128]{2,1,0:T(8,128)(2,1)S(1)} all-to-all(bf16[32,32,128]{2,1,0:T(8,128)(2,1)S(1)} %shard_map.104), channel_id=1, replica_groups=mesh['section'=8,'tp'=32] {'tp'}, dimensions={0} | all-to-all | bytes 524288 | tf_op jit(solution)/shard_map/all_to_all | solution.py:324
  63.8 0.0 copy-done.1
  63.8 2.7 %shard_map.105 = (bf16[32,32,128]{2,1,0:T(8,128)(2,1)S(1)}, bf16[24,256]{1,0:T(8,128)(2,1)}) custom-call(bf16[32,32,128]{2,1,0:T(8,128)(2,1)S(1)} %all_to_all.20.slots_ref, s32[1,24]{1,0:T(1,128)S(1)} %copy-done.1, bf16[12,32,1024]{2,1,0:T(8,128)(2,1)S(1)} %dynamic-slice_bitcast_fusion.rest_2_.keys_own, bf16[24,32,1024]{2,1,0:T(8,128)(2,1)} %bitcast.42, ...), custom_call_target="tpu_custom_call" | custom-call | tf_op jit(solution)/shard_map/pallas_call | solution.py:48
  66.5 15.5 %all_to_all.21.arrived_ref = bf16[32,32,128]{2,1,0:T(8,128)(2,1)S(1)} all-to-all(bf16[32,32,128]{2,1,0:T(8,128)(2,1)S(1)} %get-tuple-element.5), channel_id=1, replica_groups=mesh['section'=8,'tp'=32] {'tp'}, dimensions={0} | all-to-all | bytes 524288 | tf_op jit(solution)/shard_map/all_to_all | solution.py:351
  82.0 0.5 shard_map.106
  82.6 0.0 collective-permute-start.5
  82.6 4.3 %collective-permute-done.5 = bf16[24,256]{1,0:T(8,128)(2,1)S(1)} collective-permute-done((bf16[24,256]{1,0:T(8,128)(2,1)S(1)}, bf16[24,256]{1,0:T(8,128)(2,1)S(1)}, u32[]{:S(2)}, u32[]{:S(2)}) %collective-permute-start.5) | collective-permute-done | bytes 12320 | tf_op jit(solution)/shard_map/ppermute | solution.py:36
  86.9 0.6 copy.21
  (12 shorter events, 0.2 us)
Async XLA Ops:
  0.6 31.1 %copy-start = (bf16[1,1,64,10240]{3,2,1,0:T(8,128)(2,1)S(1)}, bf16[1,1,64,10240]{3,2,1,0:T(8,128)(2,1)}, u32[]{:S(2)}) copy-start(bf16[1,1,64,10240]{3,2,1,0:T(8,128)(2,1)} %param.13) | copy-start | bytes 3932164
  0.6 41.4 %collective-permute-start.2 = (bf16[24,256]{1,0:T(8,128)(2,1)}, bf16[24,256]{1,0:T(8,128)(2,1)S(1)}, u32[]{:S(2)}, u32[]{:S(2)}) collective-permute-start(bf16[24,256]{1,0:T(8,128)(2,1)} %bitcast.46), channel_id=1, source_target_pairs={{0,32},{32,64},{64,96},{96,128},{128,160},{160,192},{192,224},{224... | collective-permute-start | bytes 36872 | tf_op jit(solution)/shard_map/ppermute | solution.py:36
  2.2 27.3 %all-to-all-start = ((bf16[32,24,256]{2,1,0:T(8,128)(2,1)}), bf16[32,24,256]{2,1,0:T(8,128)(2,1)S(1)}, u32[]{:S(2)}, u32[]{:S(2)}) async-start(bf16[32,24,256]{2,1,0:T(8,128)(2,1)} %broadcast_in_dim.9), calls=%async_computation | async-start | bytes 786432 | tf_op jit(solution)/shard_map/all_to_all | solution.py:296
  13.6 5.2 %copy-start.2 = (bf16[1,24,32,1024]{3,2,1,0:T(8,128)(2,1)S(1)}, bf16[1,24,32,1024]{3,2,1,0:T(8,128)(2,1)}, u32[]{:S(2)}) copy-start(bf16[1,24,32,1024]{3,2,1,0:T(8,128)(2,1)} %param.15) | copy-start | bytes 4718596
  13.7 7.9 %copy-start.4 = (s32[1,24,1]{1,2,0:T(1,128)S(1)}, s32[1,24,1]{1,2,0:T(1,128)}, u32[]{:S(2)}) copy-start(s32[1,24,1]{1,2,0:T(1,128)} %param.16) | copy-start | bytes 292
  13.7 7.9 %copy-start.3 = (f32[8192]{0:T(1024)S(1)}, f32[8192]{0:T(1024)}, u32[]{:S(2)}) copy-start(f32[8192]{0:T(1024)} %param.10) | copy-start | bytes 98308
  15.9 26.2 %collective-permute-start.1 = (bf16[6,32,1024]{2,1,0:T(8,128)(2,1)}, bf16[6,32,1024]{2,1,0:T(8,128)(2,1)S(1)}, u32[]{:S(2)}, u32[]{:S(2)}) collective-permute-start(bf16[6,32,1024]{2,1,0:T(8,128)(2,1)} %get-tuple-element.8), channel_id=1, source_target_pairs={{0,24},{1,25},{2,26},{3,27},{4,28},{5,29},{6,30},{7,31},{8,16},{9,... | collective-permute-start | bytes 1179656 | tf_op jit(solution)/shard_map/ppermute | solution.py:292
  18.6 23.4 %collective-permute-start = (bf16[6,32,1024]{2,1,0:T(8,128)(2,1)}, bf16[6,32,1024]{2,1,0:T(8,128)(2,1)S(1)}, u32[]{:S(2)}, u32[]{:S(2)}) collective-permute-start(bf16[6,32,1024]{2,1,0:T(8,128)(2,1)} %get-tuple-element.9), channel_id=1, source_target_pairs={{0,8},{1,9},{2,10},{3,11},{4,12},{5,13},{6,14},{7,15},{8,0},{9,1},... | collective-permute-start | bytes 1179656 | tf_op jit(solution)/shard_map/ppermute | solution.py:292
  19.7 22.3 %collective-permute-start.4 = (bf16[6,32,1024]{2,1,0:T(8,128)(2,1)}, bf16[6,32,1024]{2,1,0:T(8,128)(2,1)}, u32[]{:S(2)}, u32[]{:S(2)}) collective-permute-start(bf16[6,32,1024]{2,1,0:T(8,128)(2,1)} %get-tuple-element.6), channel_id=1, source_target_pairs={{0,24},{1,25},{2,26},{3,27},{4,28},{5,29},{6,30},{7,31},{8,16},{9,... | collective-permute-start | bytes 1179656 | tf_op jit(solution)/shard_map/ppermute | solution.py:292
  20.9 21.1 %collective-permute-start.3 = (bf16[6,32,1024]{2,1,0:T(8,128)(2,1)}, bf16[6,32,1024]{2,1,0:T(8,128)(2,1)}, u32[]{:S(2)}, u32[]{:S(2)}) collective-permute-start(bf16[6,32,1024]{2,1,0:T(8,128)(2,1)} %get-tuple-element.7), channel_id=1, source_target_pairs={{0,8},{1,9},{2,10},{3,11},{4,12},{5,13},{6,14},{7,15},{8,0},{9,1},... | collective-permute-start | bytes 1179656 | tf_op jit(solution)/shard_map/ppermute | solution.py:292
  32.9 14.2 %all-to-all-start.1 = ((bf16[32,8,128]{2,1,0:T(8,128)(2,1)}), bf16[32,8,128]{2,1,0:T(8,128)(2,1)S(1)}, u32[]{:S(2)}, u32[]{:S(2)}) async-start(bf16[32,8,128]{2,1,0:T(8,128)(2,1)} %pad.14), calls=%async_computation.1 | async-start | bytes 131072 | tf_op jit(solution)/shard_map/all_to_all | solution.py:310
  42.0 21.8 %copy-start.1 = (s32[1,24]{1,0:T(1,128)S(1)}, s32[1,24]{1,0:T(1,128)}, u32[]{:S(2)}) copy-start(s32[1,24]{1,0:T(1,128)} %used_ref.1) | copy-start | bytes 292
  82.6 4.3 %collective-permute-start.5 = (bf16[24,256]{1,0:T(8,128)(2,1)S(1)}, bf16[24,256]{1,0:T(8,128)(2,1)S(1)}, u32[]{:S(2)}, u32[]{:S(2)}) collective-permute-start(bf16[24,256]{1,0:T(8,128)(2,1)S(1)} %convert_element_type.55), channel_id=1, source_target_pairs={{0,32},{32,64},{64,96},{96,128},{128,160},{160,192},{192,224},{224... | collective-permute-start | bytes 36872 | tf_op jit(solution)/shard_map/ppermute | solution.py:36
